TPU v7x, 32 devices: a whole 2x2x4 slice. The times are simulated.
32 devices in a mesh: seq: 8 (over y, x, core), head: 4 (over z).
Axes of the slice: x: 2, y: 2, z: 4, core: 2. Of those that a mesh axis runs over, the one named last changes fastest.
Arguments:
- tokens: bfloat16 [65536, 512], P(('seq', 'head')), may hold values from -6 to 6
- seq_lengths: int32 [8, 16], P('seq'), may hold values from 0 to 1024, as said below
- ln1_gain: float32 [512], replicated, may hold values from 0.5 to 1.5
- ln1_bias: float32 [512], replicated, may hold values from -3 to 3
- w_qkv: bfloat16 [512, 1536], replicated, may hold values from -0.375 to 0.375
- w_out: bfloat16 [512, 512], replicated, may hold values from -1 to 1
- w_gate1: bfloat16 [512, 512], replicated, may hold values from -0.25 to 0.25
- gate1_gain: float32 [512], replicated, may hold values from 0.5 to 2
- gate1_shift: float32 [512], replicated, may hold values from -3 to 3
- ln2_gain: float32 [512], replicated, may hold values from 0.5 to 1.5
- ln2_bias: float32 [512], replicated, may hold values from -3 to 3
- w_up: bfloat16 [512, 2048], replicated, may hold values from -0.25 to 0.25
- b_up: float32 [2048], replicated, may hold values from -3 to 3
- w_down: bfloat16 [2048, 512], replicated, may hold values from -0.1875 to 0.1875
- b_down: float32 [512], replicated, may hold values from -3 to 3
- w_gate2: bfloat16 [512, 512], replicated, may hold values from -0.25 to 0.25
- gate2_gain: float32 [512], replicated, may hold values from 0.5 to 2
- gate2_shift: float32 [512], replicated, may hold values from -3 to 3
- cotangent: bfloat16 [65536, 512], P(('seq', 'head')), may hold values from -6 to 6
Outputs:
- output: bfloat16 [65536, 512], P(('seq', 'head'))
- grad_tokens: float32 [65536, 512], P(('seq', 'head'))
- g_ln1_gain: float32 [512], replicated
- g_ln1_bias: float32 [512], replicated
- g_w_qkv: float32 [512, 1536], replicated
- g_w_out: float32 [512, 512], replicated
- g_w_gate1: float32 [512, 512], replicated
- g_gate1_gain: float32 [512], replicated
- g_gate1_shift: float32 [512], replicated
- g_ln2_gain: float32 [512], replicated
- g_ln2_bias: float32 [512], replicated
- g_w_up: float32 [512, 2048], replicated
- g_b_up: float32 [2048], replicated
- g_w_down: float32 [2048, 512], replicated
- g_b_down: float32 [512], replicated
- g_w_gate2: float32 [512, 512], replicated
- g_gate2_gain: float32 [512], replicated
- g_gate2_shift: float32 [512], replicated
Inputs may be any that keep to these rules, and one draw needn't show every extreme that they name: `seq_lengths`: each row lists the lengths of its group's sequences in order, each 512 or 1024, the two lengths mixed in any order within a group, followed by zeros; each row sums to 8192.
All inputs are finite; a program needn't handle non-finite values.
Results may differ from a plain program's by a relative error of at most 0.013.
The roundings to bfloat16 on the way count: a program that leaves them out, or rounds other values in their place, can miss the bound.
Values may be sent and summed in bfloat16 or wider, within the bound.
No kernel may reach another device: no remote copies, remote signals or barrier semaphores. Data moves between devices by JAX's collectives and lax.ppermute only.
A program may use at most 256 MiB of HBM per device.

v0:
```python
import functools

import jax
import jax.numpy as jnp
from jax import lax
from jax.experimental import pallas as pl
from jax.experimental.pallas import tpu as pltpu
from jax.sharding import PartitionSpec as P

HD = 64
SPAN = 512
TILE = 1024
MID_TILE = 512
HALF = 256
PAIR = 128
PAD = 128
LATE_WEIGHT = 0.02
EPS = 1e-05
MASKED = -1e30
SCALE = 0.125
AXES = ("seq", "head")
MIB = 1024 * 1024
VMEM_MIB = 60

F32 = jnp.float32
BF16 = jnp.bfloat16


def dot(a, b):
    return jnp.dot(a, b, preferred_element_type=F32)


def dot_nt(a, b):
    return lax.dot_general(a, b, (((1,), (1,)), ((), ())), preferred_element_type=F32)


def dot_tn(a, b):
    return lax.dot_general(a, b, (((0,), (0,)), ((), ())), preferred_element_type=F32)


def struct(shape, dtype):
    return jax.ShapeDtypeStruct(shape, dtype)


def params(mib):
    return pltpu.CompilerParams(vmem_limit_bytes=mib * MIB, dimension_semantics=("arbitrary",))


def cost(flops, nbytes, trans=0):
    return pl.CostEstimate(flops=int(flops), bytes_accessed=int(nbytes), transcendentals=int(trans))


def rows_of(width, tile=TILE):
    return pl.BlockSpec((tile, width), lambda i: (i, 0))


def whole(shape):
    return pl.BlockSpec(shape, lambda *_: (0,) * len(shape))


def normed(v):
    centered = v - jnp.mean(v, axis=-1, keepdims=True)
    rstd = lax.rsqrt(jnp.mean(centered * centered, axis=-1, keepdims=True) + EPS)
    return centered * rstd, rstd


def row(ref):
    return ref[...].reshape(1, -1)


def sigmoid(v):
    return 0.5 + 0.5 * jnp.tanh(0.5 * v)


def column_sum(v):
    return jnp.sum(v, axis=0, keepdims=True)


def add_stats(acc, z, i):
    n = z.shape[0]
    mean = column_sum(z) * (1.0 / n)
    c = z - mean
    dev = column_sum(c * c)

    @pl.when(i == 0)
    def _():
        acc[0:1, :] = mean
        acc[1:2, :] = dev

    @pl.when(i > 0)
    def _():
        before = i.astype(F32)
        gap = mean - acc[0:1, :]
        acc[0:1, :] += gap / (before + 1.0)
        acc[1:2, :] += dev + gap * gap * (n * before / (before + 1.0))


def add_sums(acc, sums, i):
    for j, s in enumerate(sums):

        @pl.when(i == 0)
        def _(j=j, s=s):
            acc[j : j + 1, :] = s

        @pl.when(i > 0)
        def _(j=j, s=s):
            acc[j : j + 1, :] += s


def spread(acc, out):
    out[...] = jnp.broadcast_to(acc[...][None], out.shape)


def merge_stats(parts, rows):
    n = parts.shape[0]
    means = parts[:, 0, :]
    mean = jnp.mean(means, axis=0, keepdims=True)
    gaps = means - mean
    dev = jnp.sum(parts[:, 1, :], axis=0, keepdims=True) + rows * jnp.sum(
        gaps * gaps, axis=0, keepdims=True
    )
    return mean, lax.rsqrt(dev * (1.0 / (rows * n)) + EPS)


def exchange(spread_rows):
    return lax.all_to_all(spread_rows, AXES, 0, 0, tiled=True)


def first_kernel(x, gain, bias, w_qkv, w_gate, h1, qkv, z1, stats, acc, z):
    i = pl.program_id(0)
    ga, bi = row(gain), row(bias)

    def norm(at):
        n, _ = normed(x[at, :].astype(F32))
        h = (n * ga + bi).astype(BF16)
        h1[at, :] = h
        return h

    def multiply(at, h):
        qkv[at, :] = dot(h, w_qkv[...]).astype(BF16)
        z[at, :] = dot(h, w_gate[...])

    staged(halves_of(x), norm, multiply)
    z1[...] = z[...].astype(BF16)
    add_stats(acc, z[...], i)

    @pl.when(i == pl.num_programs(0) - 1)
    def _():
        spread(acc, stats)


def halves_of(ref):
    step = min(HALF, ref.shape[0] // 2)
    return [slice(j, j + step) for j in range(0, ref.shape[0], step)]


def attend_kernel(flags, qkv, prev, x, gain, bias, w_qkv, out, lse, halo, kvp):
    b = pl.program_id(0)
    width = out.shape[1]
    wide = flags[b] > 0

    @pl.when(wide & (b == 0))
    def _():
        n, _ = normed(x[...].astype(F32))
        h = (n * row(gain) + row(bias)).astype(BF16)
        kvp[...] = dot(h, w_qkv[:, width:]).astype(BF16)
        halo[...] = kvp[...]

    @pl.when(wide & (b > 0))
    def _():
        kvp[...] = prev[:, width:]

    low = lax.broadcasted_iota(jnp.int32, (1, PAIR), 1) < HD
    keys_at = lax.broadcasted_iota(jnp.int32, (SPAN, SPAN), 0)
    allowed = keys_at <= lax.broadcasted_iota(jnp.int32, (SPAN, SPAN), 1)

    def compute(wide):
        turned = {}

        def scores(p, s):
            q_s = pick_head(qkv[:, p * PAIR : (p + 1) * PAIR], s, low) * jnp.asarray(SCALE, BF16)
            at = slice(width + p * PAIR, width + (p + 1) * PAIR)
            res = [jnp.where(allowed, dot_nt(qkv[:, at], q_s), MASKED)]
            if wide:
                res.append(dot_nt(kvp[:, p * PAIR : (p + 1) * PAIR], q_s))
            return res

        def finish(p, s, res):
            if p not in turned:
                v_at = slice(2 * width + p * PAIR, 2 * width + (p + 1) * PAIR)
                turned[p] = [qkv[:, v_at].T]
                if wide:
                    turned[p].append(kvp[:, width + p * PAIR : width + (p + 1) * PAIR].T)
            top = functools.reduce(
                jnp.maximum, [jnp.max(x, axis=0, keepdims=True) for x in res]
            )
            total, acc = 0.0, 0.0
            for x, vt in zip(res, turned[p]):
                e = jnp.exp(x - top)
                total = total + jnp.sum(e, axis=0, keepdims=True)
                acc = acc + dot(vt[s * HD : (s + 1) * HD], e.astype(BF16))
            lse[p, s : s + 1, :] = top + jnp.log(total)
            return acc * (1.0 / total)

        kept = {}

        def end(unit, res):
            p, s = unit
            kept[s] = finish(p, s, res)
            if s == 1:
                both = jnp.concatenate([kept[0], kept[1]], axis=0)
                out[:, p * PAIR : (p + 1) * PAIR] = both.T.astype(BF16)

        in_turn([(p, s) for p in range(width // PAIR) for s in range(2)], lambda u: scores(*u), end)

    pl.when(wide)(functools.partial(compute, True))
    pl.when(jnp.logical_not(wide))(functools.partial(compute, False))


def pick_head(v, s, low):
    return jnp.where(low if s == 0 else ~low, v, jnp.zeros_like(v))


def staged(units, *stages):
    held = [None] * len(units)
    for t in range(len(units) + len(stages) - 1):
        for k, stage in enumerate(stages):
            if 0 <= t - k < len(units):
                u = t - k
                held[u] = stage(units[u]) if k == 0 else stage(units[u], held[u])


def in_turn(units, first, second):
    held = None
    for u in units:
        got = first(u)
        if held is not None:
            second(*held)
        held = (u, got)
    second(*held)


def mix_kernel(
    rows, att, x, z1, parts, gain, shift, ln_gain, ln_bias, w_out, w_gate, y1, h2, z2, stats, acc, st
):
    i = pl.program_id(0)

    @pl.when(i == 0)
    def _():
        mean, rstd = merge_stats(parts, rows)
        st[0:1, :] = mean
        st[1:2, :] = rstd

    mean, rstd = st[0:1, :], st[1:2, :]
    ga, sh, lg, lb = row(gain), row(shift), row(ln_gain), row(ln_bias)

    def project(at):
        return dot(att[at, :], w_out[...])

    def combine(at, branch):
        t = sigmoid((z1[at, :].astype(F32) - mean) * rstd * ga + sh)
        y = t * branch + (1.0 - t) * x[at, :].astype(F32)
        y1[at, :] = y
        n, _ = normed(y)
        h = (n * lg + lb).astype(BF16)
        h2[at, :] = h
        return h

    def gate(at, h):
        z2[at, :] = dot(h, w_gate[...])

    staged(halves_of(att), project, combine, gate)
    add_stats(acc, z2[...], i)

    @pl.when(i == pl.num_programs(0) - 1)
    def _():
        spread(acc, stats)


GELU_C = 0.7978845608028654
GELU_A = 0.044715


def mlp_kernel(h2, w_up, b_up, w_down, b_down, act, slope, mlp):
    units = w_up.shape[1]
    step = 512
    bias, bias_down = row(b_up), row(b_down)

    def up(u):
        rows, j = u
        at = slice(j * step, (j + 1) * step)
        return dot(h2[rows, :], w_up[:, at])

    def curve(u, pre):
        rows, j = u
        at = slice(j * step, (j + 1) * step)
        pre = pre + bias[:, at]
        bend = GELU_C + (GELU_C * GELU_A) * (pre * pre)
        half = 0.5 * jnp.tanh(pre * bend)
        cdf = 0.5 + half
        a = pre * cdf
        act[rows, at] = a.astype(BF16)
        slope[rows, at] = (cdf + a * (0.5 - half) * (6.0 * bend - 4.0 * GELU_C)).astype(BF16)

    def down(u, _):
        rows, j = u
        if j == units // step - 1:
            mlp[rows, :] = dot(act[rows, :], w_down[...]) + bias_down

    staged([(r, j) for r in halves_of(h2) for j in range(units // step)], up, curve, down)


def gate2_kernel(rows, mlp, y1, z2, c, parts, gain, shift, out, dmlp, sums, acc, st):
    i = pl.program_id(0)

    @pl.when(i == 0)
    def _():
        mean, rstd = merge_stats(parts, rows)
        st[0:1, :] = mean
        st[1:2, :] = rstd

    nhat = (z2[...] - st[0:1, :]) * st[1:2, :]
    t = sigmoid(nhat * row(gain) + row(shift))
    m, y = mlp[...], y1[...]
    out[...] = (t * m + (1.0 - t) * y).astype(BF16)
    g = c[...].astype(F32)
    dmlp[...] = (g * t).astype(BF16)
    du = g * (m - y) * t * (1.0 - t)
    add_sums(acc, [column_sum(du), column_sum(du * nhat)], i)

    @pl.when(i == pl.num_programs(0) - 1)
    def _():
        spread(acc, sums)


def mlp_back_kernel(
    core, dmlp, act, slope, h2, w_up, w_down, dh2, keep, send, g_b, acc_up, acc_down
):
    i = pl.program_id(0)

    @pl.when(i == 0)
    def _():
        acc_up[...] = jnp.zeros_like(acc_up)
        acc_down[...] = jnp.zeros_like(acc_down)
        g_b[...] = jnp.zeros_like(g_b)

    d, h = dmlp[...], h2[...]
    units = w_up.shape[1]
    total = 0.0
    width = d.shape[1]
    steps = units // width
    for j in range(steps):
        at = slice(j * width, (j + 1) * width)
        dp = (dot_nt(d, w_down[at, :]) * slope[:, at].astype(F32)).astype(BF16)
        g_b[1 + j : 2 + j, :] += column_sum(dp.astype(F32))
        total = total + dot_nt(dp, w_up[:, at])
        acc_up[at, :] += dot_tn(h, dp)
        acc_down[:, at] += dot_tn(d, act[:, at])
    dh2[...] = total.astype(BF16)
    g_b[0:1, :] += column_sum(d.astype(F32))

    @pl.when(i == pl.num_programs(0) - 1)
    def _():
        for j in range(steps):
            at = slice(j * width, (j + 1) * width)
            half, row0 = (2 * j) // steps, (j % (steps // 2)) * width
            to = slice(row0, row0 + width)
            for out, mine in ((keep, core[0] == half), (send, core[0] != half)):

                @pl.when(mine)
                def _(out=out, at=at, to=to):
                    out[0, to, :] = acc_up[at, :].astype(BF16)
                    out[1, to, :] = acc_down[:, at].T.astype(BF16)


def middle_kernel(
    rows,
    c,
    mlp,
    y1,
    z2,
    dh2p,
    att,
    x,
    z1,
    h2,
    parts2,
    sums2,
    parts1,
    gain2,
    shift2,
    gain1,
    shift1,
    ln_gain,
    g_b,
    w_gate2,
    w_out,
    gx,
    du1,
    datt,
    delta,
    g_w,
    sums,
    g_gate2,
    side,
    acc,
    st,
    acc_gate,
    acc_out,
    dz2,
    dbranch,
):
    i = pl.program_id(0)
    count = 1.0 / (rows * parts2.shape[0])
    width = y1.shape[1]

    @pl.when(i == 0)
    def _():
        mean, rstd = merge_stats(parts2, rows)
        st[0:1, :] = mean
        st[1:2, :] = rstd
        mean, rstd = merge_stats(parts1, rows)
        st[2:3, :] = mean
        st[3:4, :] = rstd
        st[4:5, :] = jnp.sum(sums2[:, 0, :], axis=0, keepdims=True)
        st[5:6, :] = jnp.sum(sums2[:, 1, :], axis=0, keepdims=True)
        g_gate2[...] = st[4:6, :]
        acc_gate[...] = jnp.zeros_like(acc_gate)
        acc_out[...] = jnp.zeros_like(acc_out)

    ga2, sh2, ga1, sh1, lg = row(gain2), row(shift2), row(gain1), row(shift1), row(ln_gain)
    mean2, rstd2, mean1, rstd1 = [st[j : j + 1, :] for j in range(4)]
    shift_mean, gain_mean = st[4:5, :] * count, st[5:6, :] * count
    heads = width // HD
    pick = (
        lax.broadcasted_iota(jnp.int32, (heads, width), 1) // HD
        == lax.broadcasted_iota(jnp.int32, (heads, width), 0)
    ).astype(BF16)
    sums_of = []

    def gate(at):
        g = c[at, :].astype(F32)
        nhat = (z2[at, :] - mean2) * rstd2
        t = sigmoid(nhat * ga2 + sh2)
        rest = g * (1.0 - t)
        du = (rest * t) * (mlp[at, :] - y1[at, :])
        dz2[at, :] = ((ga2 * rstd2) * (du - shift_mean - nhat * gain_mean)).astype(BF16)
        return rest

    def project(at, rest):
        return rest, dot_nt(dz2[at, :], w_gate2[...]), dot(att[at, :], w_out[...])

    def norm(at, held):
        rest, back, branch = held
        dh2 = dh2p[at, :].astype(F32) + back
        n, r = normed(y1[at, :])
        e = dh2 * lg
        dy = rest + r * (
            e - jnp.mean(e, axis=-1, keepdims=True) - n * jnp.mean(e * n, axis=-1, keepdims=True)
        )
        nhat = (z1[at, :].astype(F32) - mean1) * rstd1
        t = sigmoid(nhat * ga1 + sh1)
        dyt = dy * t
        dbranch[at, :] = dyt.astype(BF16)
        out = dy - dyt
        gx[at, :] = out
        du = (out * t) * (branch - x[at, :].astype(F32))
        du1[at, :] = du.astype(BF16)
        sums_of.append(
            [column_sum(du), column_sum(du * nhat), column_sum(dh2 * n), column_sum(dh2)]
        )

    def attended(at, _):
        return dot_nt(dbranch[at, :], w_out[...])

    def finish(at, da):
        da = da.astype(BF16)
        datt[at, :] = da
        prod = da.astype(F32) * att[at, :].astype(F32)
        hi = prod.astype(BF16)
        lo = (prod - hi.astype(F32)).astype(BF16)
        dl = dot_nt(pick, hi) + dot_nt(pick, lo)
        for p in range(heads // 2):
            delta[p, :, at] = dl[2 * p : 2 * p + 2, :]

    staged(halves_of(att), gate, project, norm, attended, finish)
    acc_gate[...] += dot_tn(h2[...], dz2[...])
    acc_out[...] += dot_tn(att[...], dbranch[...])
    add_sums(acc, [sum(v) for v in zip(*sums_of)], i)

    @pl.when(i == pl.num_programs(0) - 1)
    def _():
        spread(acc.at[0:2, :], sums)
        side[0:2, :] = acc[2:4, :]
        side[2:, :] = g_b[...]
        g_w[0] = acc_gate[...].astype(BF16)
        g_w[1] = acc_out[...].astype(BF16)


def back_block(q_ref, k_ref, v_ref, do, lse, delta, kp_ref, vp_ref, wide, own, carry, dq_t):
    width = do.shape[1]
    low = lax.broadcasted_iota(jnp.int32, (1, PAIR), 1) < HD
    mask = lax.broadcasted_iota(jnp.int32, (HALF, HALF), 0) <= lax.broadcasted_iota(
        jnp.int32, (HALF, HALF), 1
    )
    full = slice(0, SPAN)
    parts = [(slice(0, HALF), full), (slice(HALF, SPAN), slice(HALF, SPAN))]
    units = []
    for p in range(width // PAIR):
        for s in range(2):
            units += [(p, s, 0), (p, s, 1)] + ([(p, s, 2)] if wide else [])
    held = {}

    def inputs(p):
        if p not in held:
            held.clear()
            at = slice(p * PAIR, (p + 1) * PAIR)
            q, d, k, v = q_ref[:, at], do[:, at], k_ref[:, at], v_ref[:, at]
            scale = jnp.asarray(SCALE, BF16)
            e = {
                "q": [pick_head(q, s, low) * scale for s in range(2)],
                "do": [pick_head(d, s, low) for s in range(2)],
                "own": (k, v, k.T * scale),
            }
            if wide:
                kp, vp = kp_ref[:, at], vp_ref[:, at]
                e["before"] = (kp, vp, kp.T * scale)
            held[p] = e
        return held[p]

    def first(unit):
        p, s, i = unit
        e = inputs(p)
        ks, qs = (full, full) if i == 2 else parts[i]
        k, v, kt = e["before"] if i == 2 else e["own"]
        q_s, d_s = e["q"][s][qs], e["do"][s][qs]
        kt = kt[s * HD : (s + 1) * HD, ks]
        return dot_nt(k[ks], q_s), dot_nt(v[ks], d_s), q_s, d_s, kt, ks, qs

    def second(unit, got):
        p, s, i = unit
        scores, dp, q_s, d_s, kt, ks, qs = got
        at = slice(p * PAIR, (p + 1) * PAIR)
        x = jnp.exp(scores - lse[p, s : s + 1, qs])
        if i == 0:
            x = jnp.concatenate([jnp.where(mask, x[:, :HALF], 0.0), x[:, HALF:]], axis=1)
        elif i == 1:
            x = jnp.where(mask, x, 0.0)
        ds = (x * (dp - delta[p, s : s + 1, qs])).astype(BF16)
        dk, dv, dq = dot(ds, q_s), dot(x.astype(BF16), d_s), dot(kt, ds)
        target = carry if i == 2 else own
        if s == 0:
            target[0, ks, at] = dk
            target[1, ks, at] = dv
        else:
            target[0, ks, at] += dk
            target[1, ks, at] += dv
        head = slice(p * PAIR + s * HD, p * PAIR + (s + 1) * HD)
        if i == 0:
            dq_t[head, :] = dq
        else:
            dq_t[head, qs] += dq

    in_turn(units, first, second)


def back_first_kernel(flags, q, k, v, do, kp, vp, lse, delta, dq, own, terms, dq_t, carry):
    wide = flags[0] > 0

    @pl.when(wide)
    def _():
        back_block(q, k, v, do, lse, delta, kp, vp, True, own, carry, dq_t)
        terms[...] = carry[...].astype(BF16)

    @pl.when(jnp.logical_not(wide))
    def _():
        back_block(q, k, v, do, lse, delta, kp, vp, False, own, carry, dq_t)
        terms[...] = jnp.zeros_like(terms)

    dq[...] = dq_t[...].T.astype(BF16)


def back_rest_kernel(
    flags, q, k, v, do, kp, vp, lse, delta, dq0, own0, dq, dk, dv, last, dq_t, carry, own
):
    j = pl.program_id(0)
    b = pl.num_programs(0) - 1 - j
    now = lax.rem(j, 2)

    @pl.when(b > 0)
    def _():
        later = carry.at[1 - now]
        wide = flags[b] > 0

        @pl.when(wide)
        def _():
            back_block(q, k, v, do, lse, delta, kp, vp, True, own, later, dq_t)

        @pl.when(jnp.logical_not(wide))
        def _():
            back_block(q, k, v, do, lse, delta, kp, vp, False, own, later, dq_t)
            later[...] = jnp.zeros_like(later)

        @pl.when(j == 0)
        def _():
            last[...] = own[...]

        @pl.when(j > 0)
        def _():
            dk[...] = (own[0] + carry[now, 0]).astype(BF16)
            dv[...] = (own[1] + carry[now, 1]).astype(BF16)

        dq[...] = dq_t[...].T.astype(BF16)

    @pl.when(b == 0)
    def _():
        dq[...] = dq0[...]
        dk[...] = (own0[0] + carry[now, 0]).astype(BF16)
        dv[...] = (own0[1] + carry[now, 1]).astype(BF16)


def last_kernel(
    rows,
    core,
    h1,
    dq_a,
    dk_a,
    dv_a,
    last_a,
    dq_b,
    dk_b,
    dv_b,
    last_b,
    arrived,
    du1,
    z1,
    parts1,
    sums1,
    gain1,
    g_mid,
    side,
    x,
    gx,
    ln_gain,
    w_qkv,
    w_gate1,
    grad_x,
    keep,
    send,
    g_sums,
    acc,
    st,
    dqkv,
    ln_sums,
):
    i = pl.program_id(0)
    final = i == pl.num_programs(0) - 1
    count = 1.0 / (rows * parts1.shape[0])
    width = h1.shape[1]

    @pl.when(i == 0)
    def _():
        mean, rstd = merge_stats(parts1, rows)
        st[2:3, :] = mean
        st[3:4, :] = rstd
        for j in range(sums1.shape[1]):
            g_sums[j : j + 1, :] = jnp.sum(sums1[:, j, :], axis=0, keepdims=True)
        acc[...] = jnp.zeros_like(acc)

    nhat = (z1[...].astype(F32) - st[2:3, :]) * st[3:4, :]
    dz = (
        (row(gain1) * st[3:4, :])
        * (du1[...].astype(F32) - g_sums[0:1, :] * count - nhat * (g_sums[1:2, :] * count))
    ).astype(BF16)

    half = dq_a.shape[1]
    dqkv[:, :half] = dq_a[...]
    dqkv[:, half:width] = dq_b[...]

    @pl.when(jnp.logical_not(final))
    def _():
        dqkv[:, width : width + half] = dk_a[...]
        dqkv[:, width + half : 2 * width] = dk_b[...]
        dqkv[:, 2 * width : 2 * width + half] = dv_a[...]
        dqkv[:, 2 * width + half :] = dv_b[...]

    @pl.when(final)
    def _():
        for j in range(2):
            for c, own in enumerate((last_a, last_b)):
                got = arrived[j, :, c * half : (c + 1) * half].astype(F32)
                at = (1 + j) * width + c * half
                dqkv[:, at : at + half] = (own[j] + got).astype(BF16)

    ht = h1[...].T
    lg = row(ln_gain)
    sums_of = []

    def back(at):
        return dot_nt(dqkv[at, :], w_qkv[...]) + dot_nt(dz[at, :], w_gate1[...])

    def weigh(at, dh):
        for j in range(4):
            if (j >= 2) == (at.start > 0):
                acc[j] += dot(ht, dz if j == 3 else dqkv[:, j * width : (j + 1) * width])
        return dh

    def norm(at, dh):
        n, r = normed(x[at, :].astype(F32))
        e = dh * lg
        grad_x[at, :] = gx[at, :] + r * (
            e - jnp.mean(e, axis=-1, keepdims=True) - n * jnp.mean(e * n, axis=-1, keepdims=True)
        )
        sums_of.append([column_sum(dh * n), column_sum(dh)])

    staged(halves_of(x), back, weigh, norm)
    add_sums(ln_sums, [sum(v) for v in zip(*sums_of)], i)

    @pl.when(final)
    def _():
        mine, other = pl.ds(core[0] * HALF, HALF), pl.ds((1 - core[0]) * HALF, HALF)
        for out, at in ((keep, mine), (send, other)):
            for j in range(4):
                out[j // 2, (j % 2) * HALF : (j % 2 + 1) * HALF, :] = acc[j, at, :].astype(BF16)
            for j in range(2):
                out[j, 2 * HALF : 3 * HALF, :] = g_mid[j, at, :]
                out[j, 3 * HALF :, :] = jnp.zeros((PAD, width), BF16)
        extra = side.shape[0]
        for out, mine in ((keep, core[0] == 0), (send, core[0] != 0)):

            @pl.when(mine)
            def _(out=out):
                out[0, 3 * HALF : 3 * HALF + 16, :] = jnp.concatenate(
                    [ln_sums[...], side[...], jnp.zeros((14 - extra, width), F32)], axis=0
                ).astype(BF16)


def mlp_out_kernel(core, mine, other, g_up, g_down):
    j = pl.program_id(0)
    half = (2 * j) // pl.num_programs(0)
    part = jnp.where(half == core[0], mine[...], other[...]).astype(F32)
    g_up[...] = part[0]
    g_down[...] = part[1]


def rest_out_kernel(core, mine, other, g_qkv, g_gate1, g_out, g_gate2, *vectors):
    width = g_out.shape[1]
    places = (
        ((g_qkv, 0), (g_qkv, 1), (g_gate2, 0)),
        ((g_qkv, 2), (g_gate1, 0), (g_out, 0)),
    )
    for ref, half in ((mine, core[0]), (other, 1 - core[0])):
        at = pl.ds(pl.multiple_of(half * HALF, HALF), HALF)
        for lane, row_places in enumerate(places):
            for j, (out, column) in enumerate(row_places):
                out[at, column * width : (column + 1) * width] = ref[
                    lane, j * HALF : (j + 1) * HALF, :
                ].astype(F32)
    a = mine[0, 3 * HALF : 3 * HALF + 16, :].astype(F32)
    b = other[0, 3 * HALF : 3 * HALF + 16, :].astype(F32)
    extra = jnp.where(core[0] == 0, a, b)
    at = 0
    for out in vectors:
        for j in range(out.shape[0] // width):
            out[j * width : (j + 1) * width] = extra[at]
            at += 1


def between_chips(x):
    seq, head = lax.axis_size("seq"), lax.axis_size("head")
    groups = [[d for d in range(seq * head) if (d // head) % 2 == c] for c in range(2)]
    return lax.all_to_all(x, AXES, 0, 0, axis_index_groups=groups, tiled=True)


def swap(x, axis, bit):
    n = lax.axis_size(axis)
    return lax.ppermute(x, axis, [(i, i ^ bit) for i in range(n)])


def upper(axis, bit):
    return (lax.axis_index(axis) & bit) // bit


def bits(axis):
    return [(axis, 1 << j) for j in range((lax.axis_size(axis) - 1).bit_length())]


class Total:
    def __init__(self, keep, send):
        near = bits("seq")
        first, layer = near[:1], near[1:]
        self.orders = [first + layer, first + layer[::-1]]
        self.far = len(near)
        self.steps = self.far + 1
        self.keep = [keep[0], keep[1]]
        self.send = send
        self.got = None
        self.at = 0

    def _swap(self, parts, stage):
        a, b = self.orders[0][stage], self.orders[1][stage]
        if a == b:
            self.stacked = jnp.stack(parts) if isinstance(parts, list) else parts
            self.both = swap(self.stacked, *a)
            return [self.both[0], self.both[1]]
        return [swap(parts[0], *a), swap(parts[1], *b)]

    def _part(self, lane, start, size):
        a = lax.dynamic_slice_in_dim(self.keep[lane], start, size, 0)
        b = lax.dynamic_slice_in_dim(self.got[lane], start, size, 0)
        return (a.astype(F32) + b.astype(F32)).astype(BF16)

    def left(self):
        return 2 * self.steps - self.at

    def parts(self):
        k, n = self.at, lax.axis_size("head")
        if k == 0:
            return self.send
        rows = self.keep[0].shape[0]
        if k < self.far:
            mine = [upper(*order[k]) for order in self.orders]
            half = rows // 2
            parts = [self._part(lane, (1 - m) * half, half) for lane, m in enumerate(mine)]
            self.keep = [self._part(lane, m * half, half) for lane, m in enumerate(mine)]
            return parts
        place = lax.axis_index("head")
        if k == self.far:
            size = rows // n

            def part(d):
                start = (place ^ d) * size
                return jnp.stack([self._part(lane, start, size) for lane in range(2)])

            parts = [part(d) for d in range(1, n)]
            self.keep = part(0)
            return parts
        if k == self.far + 1:
            total = self.keep.astype(F32)
            for v in self.got:
                total = total + v.astype(F32)
            self.keep = total.astype(BF16)
        elif k == self.far + 2:
            pieces = []
            for j in range(n):
                piece = self.keep
                for d in range(1, n):
                    piece = jnp.where((place ^ j) == d, self.got[d - 1], piece)
                pieces.append(piece)
            joined = jnp.concatenate(pieces, axis=1)
            self.keep = [joined[0], joined[1]]
        else:
            self.keep = self._joined(2 * self.steps - k)
        return self.keep

    def start(self, parts):
        k, n = self.at, lax.axis_size("head")
        if k >= self.steps:
            self.keep = parts
        if self.far <= k <= self.far + 1:
            self.got = [
                swap(parts[d - 1] if k == self.far else parts, "head", d) for d in range(1, n)
            ]
        else:
            self.got = self._swap(parts, k if k < self.far else 2 * self.steps - 1 - k)
        self.at += 1

    def _joined(self, stage):
        out = []
        for lane in range(2):
            up = upper(*self.orders[lane][stage]) > 0
            a, b = self.keep[lane], self.got[lane]
            out.append(jnp.concatenate([jnp.where(up, b, a), jnp.where(up, a, b)], axis=0))
        return out


def arrive_with(total, held):
    total.got, held = lax.optimization_barrier((total.got, held))
    return held


def joint_step(totals, held=()):
    parts, held = lax.optimization_barrier(([t.parts() for t in totals], held))
    for t, p in zip(totals, parts):
        t.start(p)
    return held


def continuation(lengths, span):
    place = jnp.arange(lengths.shape[0], dtype=jnp.int32)
    starts = jnp.sum(jnp.where(place[None, :] < place[:, None], lengths[None, :], 0), axis=1)
    begins = place * span
    hit = (starts[None, :] == begins[:, None]) & (lengths[None, :] > 0)
    return 1 - jnp.max(hit.astype(jnp.int32), axis=1)


def body(
    tokens,
    seq_lengths,
    ln1_gain,
    ln1_bias,
    w_qkv,
    w_out,
    w_gate1,
    gate1_gain,
    gate1_shift,
    ln2_gain,
    ln2_bias,
    w_up,
    b_up,
    w_down,
    b_down,
    w_gate2,
    gate2_gain,
    gate2_shift,
    cotangent,
):
    rows, width = tokens.shape
    units = w_up.shape[1]
    ndev = lax.axis_size("seq") * lax.axis_size("head")
    blocks = rows // SPAN
    pairs = width // PAIR
    heads = width // HD
    count = lax.axis_size("head")
    mac = rows * width * width

    tail = tokens[rows - SPAN :]
    before = lax.ppermute(tail, "head", [(i, i + 1) for i in range(count - 1)])
    flags = lax.dynamic_slice_in_dim(
        continuation(seq_lengths[0], SPAN), lax.axis_index("head") * blocks, blocks, 0
    )

    vec = whole((width,))
    stats_shape = (ndev, 2, width)
    h1, qkv, z1, stats1 = pl.pallas_call(
        first_kernel,
        grid=(rows // TILE,),
        in_specs=[rows_of(width), vec, vec, whole(w_qkv.shape), whole(w_gate1.shape)],
        out_specs=[rows_of(width), rows_of(3 * width), rows_of(width), whole(stats_shape)],
        out_shape=[
            struct((rows, width), BF16),
            struct((rows, 3 * width), BF16),
            struct((rows, width), BF16),
            struct(stats_shape, F32),
        ],
        scratch_shapes=[pltpu.VMEM((2, width), F32), pltpu.VMEM((TILE, width), F32)],
        compiler_params=params(VMEM_MIB),
        cost_estimate=cost(8 * mac, rows * width * 14, rows),
        name="first",
    )(tokens, ln1_gain, ln1_bias, w_qkv, w_gate1)
    parts1 = exchange(stats1)

    att, lse, kv_halo = pl.pallas_call(
        attend_kernel,
        grid_spec=pltpu.PrefetchScalarGridSpec(
            num_scalar_prefetch=1,
            grid=(blocks,),
            in_specs=[
                pl.BlockSpec((SPAN, 3 * width), lambda b, f: (b, 0)),
                pl.BlockSpec((SPAN, 3 * width), lambda b, f: (jnp.maximum(b - 1, 0), 0)),
                whole((SPAN, width)),
                vec,
                vec,
                whole(w_qkv.shape),
            ],
            out_specs=[
                pl.BlockSpec((SPAN, width), lambda b, f: (b, 0)),
                pl.BlockSpec((pairs, 2, SPAN), lambda b, f: (0, 0, b)),
                whole((SPAN, 2 * width)),
            ],
            scratch_shapes=[pltpu.VMEM((SPAN, 2 * width), BF16)],
        ),
        out_shape=[
            struct((rows, width), BF16),
            struct((pairs, 2, rows), F32),
            struct((SPAN, 2 * width), BF16),
        ],
        compiler_params=params(VMEM_MIB),
        cost_estimate=cost(10 * heads * SPAN * SPAN * PAIR * 4, 12 * MIB, heads * SPAN * SPAN * 5),
        name="attend",
    )(flags, qkv, qkv, before, ln1_gain, ln1_bias, w_qkv)

    y1, h2, z2, stats2 = pl.pallas_call(
        functools.partial(mix_kernel, rows),
        grid=(rows // TILE,),
        in_specs=[rows_of(width), rows_of(width), rows_of(width), whole(stats_shape)]
        + [vec] * 4
        + [whole(w_out.shape), whole(w_gate2.shape)],
        out_specs=[rows_of(width), rows_of(width), rows_of(width), whole(stats_shape)],
        out_shape=[
            struct((rows, width), F32),
            struct((rows, width), BF16),
            struct((rows, width), F32),
            struct(stats_shape, F32),
        ],
        scratch_shapes=[pltpu.VMEM((2, width), F32), pltpu.VMEM((8, width), F32)],
        compiler_params=params(VMEM_MIB),
        cost_estimate=cost(4 * mac, rows * width * 18, rows * width),
        name="mix",
    )(att, tokens, z1, parts1, gate1_gain, gate1_shift, ln2_gain, ln2_bias, w_out, w_gate2)
    parts2 = exchange(stats2)

    act, slope, mlp = pl.pallas_call(
        mlp_kernel,
        grid=(blocks,),
        in_specs=[
            rows_of(width, SPAN),
            whole(w_up.shape),
            whole((units,)),
            whole(w_down.shape),
            vec,
        ],
        out_specs=[rows_of(units, SPAN), rows_of(units, SPAN), rows_of(width, SPAN)],
        out_shape=[
            struct((rows, units), BF16),
            struct((rows, units), BF16),
            struct((rows, width), F32),
        ],
        compiler_params=params(VMEM_MIB),
        cost_estimate=cost(4 * rows * width * units, rows * units * 4, rows * units),
        name="mlp",
    )(h2, w_up, b_up, w_down, b_down)

    output, dmlp, sums2 = pl.pallas_call(
        functools.partial(gate2_kernel, rows),
        grid=(rows // TILE,),
        in_specs=[rows_of(width)] * 4 + [whole(stats_shape), vec, vec],
        out_specs=[rows_of(width), rows_of(width), whole(stats_shape)],
        out_shape=[
            struct((rows, width), BF16),
            struct((rows, width), BF16),
            struct(stats_shape, F32),
        ],
        scratch_shapes=[pltpu.VMEM((2, width), F32), pltpu.VMEM((8, width), F32)],
        compiler_params=params(VMEM_MIB),
        cost_estimate=cost(rows * width * 20, rows * width * 18, rows * width),
        name="gate2",
    )(mlp, y1, z2, cotangent, parts2, gate2_gain, gate2_shift)
    parts_du2 = exchange(sums2)

    bias_rows = 1 + units // width
    core = (lax.axis_index("seq") & 1).reshape(1)
    smem = pl.BlockSpec(memory_space=pltpu.SMEM)
    mlp_half = (2, units // 2, width)
    dh2p, keep, send, g_b = pl.pallas_call(
        mlp_back_kernel,
        grid=(blocks,),
        in_specs=[
            smem,
            rows_of(width, SPAN),
            rows_of(units, SPAN),
            rows_of(units, SPAN),
            rows_of(width, SPAN),
            whole(w_up.shape),
            whole(w_down.shape),
        ],
        out_specs=[
            rows_of(width, SPAN),
            whole(mlp_half),
            whole(mlp_half),
            whole((bias_rows, width)),
        ],
        out_shape=[
            struct((rows, width), BF16),
            struct(mlp_half, BF16),
            struct(mlp_half, BF16),
            struct((bias_rows, width), F32),
        ],
        scratch_shapes=[pltpu.VMEM((units, width), F32), pltpu.VMEM((width, units), F32)],
        compiler_params=params(VMEM_MIB),
        cost_estimate=cost(8 * rows * width * units, rows * units * 5),
        name="mlp_back",
    )(core, dmlp, act, slope, h2, w_up, w_down)
    keep, send, dh2p, parts_du2 = lax.optimization_barrier((keep, send, dh2p, parts_du2))
    swapped = swap(send, "seq", 1)
    chips = ndev // 2
    pair_sum = (keep.astype(F32) + swapped.astype(F32)).astype(BF16)
    pair_sum = pair_sum.reshape(chips, units // chips, width)
    pair_sum, dh2p = lax.optimization_barrier((pair_sum, dh2p))
    scattered = between_chips(pair_sum)

    mid_shape = (2, width, width)
    rows_pair = pl.BlockSpec((pairs, 2, MID_TILE), lambda i: (0, 0, i))
    side_rows = 2 + bias_rows
    gx, du1, datt, delta, g_mid, sums1, g_gate2, side = pl.pallas_call(
        functools.partial(middle_kernel, rows),
        grid=(rows // MID_TILE,),
        in_specs=[rows_of(width, MID_TILE)] * 9
        + [whole(stats_shape)] * 3
        + [vec] * 5
        + [whole((bias_rows, width)), whole(w_gate2.shape), whole(w_out.shape)],
        out_specs=[
            rows_of(width, MID_TILE),
            rows_of(width, MID_TILE),
            rows_of(width, MID_TILE),
            rows_pair,
            whole(mid_shape),
            whole(stats_shape),
            whole((2, width)),
            whole((side_rows, width)),
        ],
        out_shape=[
            struct((rows, width), F32),
            struct((rows, width), BF16),
            struct((rows, width), BF16),
            struct((pairs, 2, rows), F32),
            struct(mid_shape, BF16),
            struct(stats_shape, F32),
            struct((2, width), F32),
            struct((side_rows, width), F32),
        ],
        scratch_shapes=[
            pltpu.VMEM((4, width), F32),
            pltpu.VMEM((8, width), F32),
            pltpu.VMEM((width, width), F32),
            pltpu.VMEM((width, width), F32),
            pltpu.VMEM((MID_TILE, width), BF16),
            pltpu.VMEM((MID_TILE, width), BF16),
        ],
        compiler_params=params(VMEM_MIB),
        cost_estimate=cost(10 * mac, rows * width * 38, rows * width * 2),
        name="middle",
    )(
        cotangent,
        mlp,
        y1,
        z2,
        dh2p,
        att,
        tokens,
        z1,
        h2,
        parts2,
        parts_du2,
        parts1,
        gate2_gain,
        gate2_shift,
        gate1_gain,
        gate1_shift,
        ln2_gain,
        g_b,
        w_gate2,
        w_out,
    )

    def columns_at(j, parts=1):
        return lambda i, f: (0, j * parts)

    dq0, own0, terms = pl.pallas_call(
        back_first_kernel,
        grid_spec=pltpu.PrefetchScalarGridSpec(
            num_scalar_prefetch=1,
            grid=(1,),
            in_specs=[
                pl.BlockSpec((SPAN, width), columns_at(0)),
                pl.BlockSpec((SPAN, width), columns_at(1)),
                pl.BlockSpec((SPAN, width), columns_at(2)),
                whole((SPAN, width)),
                pl.BlockSpec((SPAN, width), columns_at(0)),
                pl.BlockSpec((SPAN, width), columns_at(1)),
                whole((pairs, 2, SPAN)),
                whole((pairs, 2, SPAN)),
            ],
            out_specs=[
                whole((SPAN, width)),
                whole((2, SPAN, width)),
                whole((2, SPAN, width)),
            ],
            scratch_shapes=[
                pltpu.VMEM((width, SPAN), F32),
                pltpu.VMEM((2, SPAN, width), F32),
            ],
        ),
        out_shape=[
            struct((SPAN, width), BF16),
            struct((2, SPAN, width), F32),
            struct((2, SPAN, width), BF16),
        ],
        compiler_params=params(VMEM_MIB),
        cost_estimate=cost(
            10 * heads * SPAN * SPAN * PAIR * 2, 8 * MIB, heads * SPAN * SPAN * 2
        ),
        name="attend_back_first",
    )(flags, qkv, qkv, qkv, datt, kv_halo, kv_halo, lse, delta)
    arrived = lax.ppermute(terms, "head", [(i + 1, i) for i in range(count - 1)])

    def block(j):
        return jnp.maximum(blocks - 1 - j, 1)

    groups = 2
    group = width // groups

    def back_rest(g, own0, weight):
        def at(column, shift=0):
            return pl.BlockSpec(
                (SPAN, group), lambda j, f: (block(j) - shift, column * groups + g)
            )

        row_block = pl.BlockSpec((pairs // groups, 2, SPAN), lambda j, f: (g, 0, block(j)))
        out_block = pl.BlockSpec((SPAN, group), lambda j, f: (blocks - 1 - j, 0))
        return pl.pallas_call(
            back_rest_kernel,
            grid_spec=pltpu.PrefetchScalarGridSpec(
                num_scalar_prefetch=1,
                grid=(blocks,),
                in_specs=[
                    at(0),
                    at(1),
                    at(2),
                    at(0),
                    at(1, 1),
                    at(2, 1),
                    row_block,
                    row_block,
                    pl.BlockSpec((SPAN, group), lambda j, f: (0, g)),
                    pl.BlockSpec((2, SPAN, group), lambda j, f: (0, 0, g)),
                ],
                out_specs=[out_block, out_block, out_block, whole((2, SPAN, group))],
                scratch_shapes=[
                    pltpu.VMEM((group, SPAN), F32),
                    pltpu.VMEM((2, 2, SPAN, group), F32),
                    pltpu.VMEM((2, SPAN, group), F32),
                ],
            ),
            out_shape=[struct((rows, group), BF16)] * 3 + [struct((2, SPAN, group), F32)],
            compiler_params=params(VMEM_MIB),
            cost_estimate=cost(
                10 * weight * heads * SPAN * SPAN * PAIR * 3,
                10 * weight * MIB,
                weight * heads * SPAN * SPAN * 2,
            ),
            name="attend_back_rest",
        )(flags, qkv, qkv, qkv, datt, qkv, qkv, lse, delta, dq0, own0)

    back_a = back_rest(0, own0, 1.0)
    back_a, scattered = lax.optimization_barrier((back_a, scattered))
    mine = jnp.sum(scattered.astype(F32), axis=0).astype(BF16)
    mine = jnp.broadcast_to(mine[None], pair_sum.shape)
    mine, own0, sums1 = lax.optimization_barrier((mine, own0, sums1))
    parts_du1 = exchange(sums1)
    back_b = back_rest(1, own0, LATE_WEIGHT)
    mine, parts_du1, back_b, arrived = lax.optimization_barrier((mine, parts_du1, back_b, arrived))
    gathered = between_chips(mine)

    in_half = (2, 3 * HALF + PAD, width)
    grouped = [rows_of(group, SPAN)] * 3 + [whole((2, SPAN, group))]
    grad_x, keep, send, g_sums = pl.pallas_call(
        functools.partial(last_kernel, rows),
        grid=(blocks,),
        in_specs=[smem, rows_of(width, SPAN)]
        + grouped * 2
        + [whole((2, SPAN, width))]
        + [rows_of(width, SPAN)] * 2
        + [whole(stats_shape), whole(stats_shape), vec, whole(mid_shape)]
        + [whole((side_rows, width))]
        + [rows_of(width, SPAN)] * 2
        + [vec, whole(w_qkv.shape), whole(w_gate1.shape)],
        out_specs=[
            rows_of(width, SPAN),
            whole(in_half),
            whole(in_half),
            whole((2, width)),
        ],
        out_shape=[
            struct((rows, width), F32),
            struct(in_half, BF16),
            struct(in_half, BF16),
            struct((2, width), F32),
        ],
        scratch_shapes=[
            pltpu.VMEM((4, width, width), F32),
            pltpu.VMEM((8, width), F32),
            pltpu.VMEM((SPAN, 3 * width), BF16),
            pltpu.VMEM((2, width), F32),
        ],
        compiler_params=params(VMEM_MIB),
        cost_estimate=cost(LATE_WEIGHT * 16 * mac, LATE_WEIGHT * rows * width * 26),
        name="last",
    )(
        core,
        h1,
        *back_a,
        *back_b,
        arrived,
        du1,
        z1,
        parts1,
        parts_du1,
        gate1_gain,
        g_mid,
        side,
        tokens,
        gx,
        ln1_gain,
        w_qkv,
        w_gate1,
    )

    total = Total(keep, send)
    while total.at < total.far:
        joint_step([total])
    gathered = joint_step([total], gathered)
    gathered = gathered.reshape(mlp_half)
    other = swap(gathered, "seq", 1)
    other, gathered = joint_step([total], (other, gathered))
    unit_rows = pl.BlockSpec((2, width, width), lambda j: (0, lax.rem(j, units // width // 2), 0))
    g_up, g_down = pl.pallas_call(
        mlp_out_kernel,
        grid=(units // width,),
        in_specs=[smem, unit_rows, unit_rows],
        out_specs=[
            pl.BlockSpec((width, width), lambda j: (0, j)),
            pl.BlockSpec((width, width), lambda j: (j, 0)),
        ],
        out_shape=[struct(w_up.shape, F32), struct(w_down.shape, F32)],
        compiler_params=params(VMEM_MIB),
        cost_estimate=cost(units * width, 12 * MIB),
        name="mlp_out",
    )(core, gathered, other)
    g_up, g_down = arrive_with(total, (g_up, g_down))
    while total.left():
        joint_step([total])
    vector = struct((width,), F32)
    (
        g_qkv,
        g_gate1,
        g_out,
        g_gate2_w,
        g_ln1_gain,
        g_ln1_bias,
        g_ln2_gain,
        g_ln2_bias,
        g_b_down,
        g_b_up,
    ) = pl.pallas_call(
        rest_out_kernel,
        in_specs=[smem] + [pl.BlockSpec(memory_space=pltpu.VMEM)] * 2,
        out_specs=[pl.BlockSpec(memory_space=pltpu.VMEM)] * 10,
        out_shape=[
            struct(w_qkv.shape, F32),
            struct(w_gate1.shape, F32),
            struct(w_out.shape, F32),
            struct(w_gate2.shape, F32),
        ]
        + [vector] * 5
        + [struct((units,), F32)],
        compiler_params=pltpu.CompilerParams(vmem_limit_bytes=VMEM_MIB * MIB),
        cost_estimate=cost(units * width, 12 * MIB),
        name="rest_out",
    )(core, total.stacked, total.both)
    return (
        output,
        grad_x,
        g_ln1_gain,
        g_ln1_bias,
        g_qkv,
        g_out,
        g_gate1,
        g_sums[1],
        g_sums[0],
        g_ln2_gain,
        g_ln2_bias,
        g_up,
        g_b_up,
        g_down,
        g_b_down,
        g_gate2_w,
        g_gate2[1],
        g_gate2[0],
    )


def solution(mesh):
    split = P(AXES, None)
    return jax.shard_map(
        body,
        mesh=mesh,
        in_specs=(split, P("seq", None)) + (P(),) * 16 + (split,),
        out_specs=(split, split) + (P(),) * 16,
        check_vma=False,
    )
```

profile of v0, /device:TPU:0, one launch (start us, length us, event | category | flops | bytes accessed | tf_op | source)
XLA Modules:
  0.0 336.2 jit_solution(10371062872246157213)
XLA Ops:
  1.7 5.0 %collective-permute-start = (bf16[512,512]{1,0:T(8,128)(2,1)S(1)}, bf16[512,512]{1,0:T(8,128)(2,1)S(1)}, u32[]{:S(2)}, u32[]{:S(2)}) collective-permute-start(bf16[512,512]{1,0:T(8,128)(2,1)S(1)} %slice.33), channel_id=1, source_target_pairs={{0,1},{1,2},{2,3},{4,5},{5,6},{6,7},{8,9},{9,10},{10,11},{12,13},{... | collective-permute-start | bytes 1572872 | tf_op jit(solution)/shard_map/ppermute | solution.py:928
  6.7 10.4 %first.1 = (bf16[2048,512]{1,0:T(8,128)(2,1)}, bf16[2048,1536]{1,0:T(8,128)(2,1)}, bf16[2048,512]{1,0:T(8,128)(2,1)}, f32[32,2,512]{2,1,0:T(2,128)}) custom-call(bf16[2048,512]{1,0:T(8,128)(2,1)} %x.7, f32[512]{0:T(512)} %ln_gain.5, f32[512]{0:T(512)} %bias.3, bf16[512,1536]{1,0:T(8,128)(2,1)} %w_qkv.5, bf16[512,512]{1,0:T(8,128)(2,1)} %w_gate1.1), custom_call_target="tpu_custom_call" | custom-call | flops 4294967296 | bytes 14680064 | tf_op jit(solution)/shard_map/first/pallas_call | solution.py:935
  17.1 5.1 %all-to-all-start = ((f32[32,2,512]{2,1,0:T(2,128)}), f32[32,2,512]{2,1,0:T(2,128)S(1)}, u32[]{:S(2)}, u32[]{:S(2)}) async-start(f32[32,2,512]{2,1,0:T(2,128)} %get-tuple-element.120), calls=%async_computation | async-start | bytes 262144 | tf_op jit(solution)/shard_map/all_to_all | solution.py:126
  23.9 21.3 %attend.1 = (bf16[2048,512]{1,0:T(8,128)(2,1)}, f32[4,2,2048]{2,1,0:T(2,128)}, bf16[512,1024]{1,0:T(8,128)(2,1)}) custom-call(s32[4]{0:T(128)} %dynamic_slice.99.flags, bf16[2048,1536]{1,0:T(8,128)(2,1)} %get-tuple-element.117.qkv.prev.q.k.v.kp.vp, bf16[2048,1536]{1,0:T(8,128)(2,1)} %get-tuple-element.117.qkv.prev.q.k.v.kp.vp, bf16[512,512]{1,0:T(8,128)(2,1)} %copy-done.11, ...), custom_call_target="tpu_custom_call" | custom-call | flops 10737418240 | bytes 12582912 | tf_op jit(solution)/shard_map/attend/pallas_call | solution.py:953
  45.9 10.5 %mix.1 = (f32[2048,512]{1,0:T(8,128)}, bf16[2048,512]{1,0:T(8,128)(2,1)}, f32[2048,512]{1,0:T(8,128)}, f32[32,2,512]{2,1,0:T(2,128)}) custom-call(bf16[2048,512]{1,0:T(8,128)(2,1)} %get-tuple-element.118.att, bf16[2048,512]{1,0:T(8,128)(2,1)} %x.7, bf16[2048,512]{1,0:T(8,128)(2,1)} %get-tuple-element.119.z1, f32[32,2,512]{2,1,0:T(2,128)} %copy-done.4, ...), custom_call_target="tpu_custom_call" | custom-call | flops 2147483648 | bytes 18874368 | tf_op jit(solution)/shard_map/mix/pallas_call | solution.py:983
  56.4 7.4 %all-to-all-start.1 = ((f32[32,2,512]{2,1,0:T(2,128)}), f32[32,2,512]{2,1,0:T(2,128)S(1)}, u32[]{:S(2)}, u32[]{:S(2)}) async-start(f32[32,2,512]{2,1,0:T(2,128)} %get-tuple-element.125), calls=%async_computation.1 | async-start | bytes 262144 | tf_op jit(solution)/shard_map/all_to_all | solution.py:126
  63.9 20.1 %mlp.1 = (bf16[2048,2048]{1,0:T(8,128)(2,1)}, bf16[2048,2048]{1,0:T(8,128)(2,1)}, f32[2048,512]{1,0:T(8,128)}) custom-call(bf16[2048,512]{1,0:T(8,128)(2,1)} %get-tuple-element.121.h2, bf16[512,2048]{1,0:T(8,128)(2,1)} %w_up.3, f32[2048]{0:T(1024)} %b_up.1, bf16[2048,512]{1,0:T(8,128)(2,1)} %w_down.3, f32[512]{0:T(512)} %b_down.1), custom_call_target="tpu_custom_call" | custom-call | flops 8589934592 | bytes 16777216 | tf_op jit(solution)/shard_map/mlp/pallas_call | solution.py:1003
  84.6 8.5 %gate2.1 = (bf16[2048,512]{1,0:T(8,128)(2,1)}, bf16[2048,512]{1,0:T(8,128)(2,1)}, f32[32,2,512]{2,1,0:T(2,128)}) custom-call(f32[2048,512]{1,0:T(8,128)} %get-tuple-element.122.mlp, f32[2048,512]{1,0:T(8,128)} %get-tuple-element.123.y1, f32[2048,512]{1,0:T(8,128)} %get-tuple-element.124.z2, bf16[2048,512]{1,0:T(8,128)(2,1)} %c.3, f32[32,2,512]{2,1,0:T(2,128)} %copy-done.5, ...), custom_call_target="tpu_custom_call" | custom-call | flops 20971520 | bytes 18874368 | tf_op jit(solution)/shard_map/gate2/pallas_call | solution.py:1024
  93.1 6.0 %all-to-all-start.2 = ((f32[32,2,512]{2,1,0:T(2,128)}), f32[32,2,512]{2,1,0:T(2,128)S(1)}, u32[]{:S(2)}, u32[]{:S(2)}) async-start(f32[32,2,512]{2,1,0:T(2,128)} %get-tuple-element.134), calls=%async_computation.2 | async-start | bytes 262144 | tf_op jit(solution)/shard_map/all_to_all | solution.py:126
  99.1 26.9 %mlp_back.1 = (bf16[2048,512]{1,0:T(8,128)(2,1)}, bf16[2,1024,512]{2,1,0:T(8,128)(2,1)}, bf16[2,1024,512]{2,1,0:T(8,128)(2,1)}, f32[5,512]{1,0:T(8,128)}) custom-call(s32[1]{0:T(128)} %bitcast.2.core, bf16[2048,512]{1,0:T(8,128)(2,1)} %get-tuple-element.128.dmlp, bf16[2048,2048]{1,0:T(8,128)(2,1)} %get-tuple-element.129.act, ...), custom_call_target="tpu_custom_call" | custom-call | flops 17179869184 | bytes 20971520 | tf_op jit(solution)/shard_map/mlp_back/pallas_call | solution.py:1045
  134.0 6.8 %all-to-all-start.3 = ((bf16[16,128,512]{2,1,0:T(8,128)(2,1)}), bf16[16,128,512]{2,1,0:T(8,128)(2,1)S(1)}, u32[]{:S(2)}, u32[]{:S(2)}) async-start(bf16[16,128,512]{2,1,0:T(8,128)(2,1)} %bitcast.3), calls=%async_computation.3 | async-start | bytes 4194304 | tf_op jit(solution)/shard_map/all_to_all | solution.py:772
  140.8 20.2 %middle.1 = (f32[2048,512]{1,0:T(8,128)}, bf16[2048,512]{1,0:T(8,128)(2,1)}, bf16[2048,512]{1,0:T(8,128)(2,1)}, f32[4,2,2048]{2,1,0:T(2,128)}, bf16[2,512,512]{2...) custom-call(bf16[2048,512]{1,0:T(8,128)(2,1)} %c.3, ...), custom_call_target="tpu_custom_call" | custom-call | flops 5368709120 | bytes 39845888 | tf_op jit(solution)/shard_map/middle/pallas_call | solution.py:1085
  161.1 8.6 %attend_back_first.1 = (bf16[512,512]{1,0:T(8,128)(2,1)}, f32[2,512,512]{2,1,0:T(8,128)}, bf16[2,512,512]{2,1,0:T(8,128)(2,1)}) custom-call(s32[4]{0:T(128)} %dynamic_slice.99.flags, bf16[2048,1536]{1,0:T(8,128)(2,1)} %get-tuple-element.117.qkv.prev.q.k.v.kp.vp, bf16[2048,1536]{1,0:T(8,128)(2,1)} %get-tuple-element.117.qkv.prev.q.k.v.kp.vp, ...), custom_call_target="tpu_custom_call" | custom-call | flops 5368709120 | bytes 8388608 | tf_op jit(solution)/shard_map/attend_back_first/pallas_call | solution.py:1149
  171.0 16.6 %attend_back_rest.2 = (bf16[2048,256]{1,0:T(8,128)(2,1)}, bf16[2048,256]{1,0:T(8,128)(2,1)}, bf16[2048,256]{1,0:T(8,128)(2,1)}, f32[2,512,256]{2,1,0:T(8,128)}) custom-call(s32[4]{0:T(128)} %dynamic_slice.99.flags, bf16[2048,1536]{1,0:T(8,128)(2,1)} %get-tuple-element.117.qkv.prev.q.k.v.kp.vp, bf16[2048,1536]{1,0:T(8,128)(2,1)} %get-tuple-element.117.qkv.prev.q.k.v.kp.vp, ...), custom_call_target="tpu_custom_call" | custom-call | flops 8053063680 | bytes 10485760 | tf_op jit(solution)/shard_map/attend_back_rest/pallas_call | solution.py:1201
  193.9 5.9 %all-to-all-start.4 = ((f32[32,2,512]{2,1,0:T(2,128)}), f32[32,2,512]{2,1,0:T(2,128)S(1)}, u32[]{:S(2)}, u32[]{:S(2)}) async-start(f32[32,2,512]{2,1,0:T(2,128)} %get-tuple-element.159), calls=%async_computation.4 | async-start | bytes 262144 | tf_op jit(solution)/shard_map/all_to_all | solution.py:126
  199.8 16.6 %attend_back_rest.3 = (bf16[2048,256]{1,0:T(8,128)(2,1)}, bf16[2048,256]{1,0:T(8,128)(2,1)}, bf16[2048,256]{1,0:T(8,128)(2,1)}, f32[2,512,256]{2,1,0:T(8,128)}) custom-call(s32[4]{0:T(128)} %dynamic_slice.99.flags, bf16[2048,1536]{1,0:T(8,128)(2,1)} %get-tuple-element.117.qkv.prev.q.k.v.kp.vp, bf16[2048,1536]{1,0:T(8,128)(2,1)} %get-tuple-element.117.qkv.prev.q.k.v.kp.vp, ...), custom_call_target="tpu_custom_call" | custom-call | flops 161061280 | bytes 209715 | tf_op jit(solution)/shard_map/attend_back_rest/pallas_call | solution.py:1201
  217.4 6.1 %all-to-all-start.5 = ((bf16[16,128,512]{2,1,0:T(8,128)(2,1)}), bf16[16,128,512]{2,1,0:T(8,128)(2,1)S(1)}, u32[]{:S(2)}, u32[]{:S(2)}) async-start(bf16[16,128,512]{2,1,0:T(8,128)(2,1)} %broadcast_in_dim.27), calls=%async_computation.5 | async-start | bytes 4194304 | tf_op jit(solution)/shard_map/all_to_all | solution.py:772
  223.5 21.0 %last.1 = (f32[2048,512]{1,0:T(8,128)}, bf16[2,896,512]{2,1,0:T(8,128)(2,1)}, bf16[2,896,512]{2,1,0:T(8,128)(2,1)}, f32[2,512]{1,0:T(2,128)}) custom-call(s32[1]{0:T(128)} %bitcast.2.core, bf16[2048,512]{1,0:T(8,128)(2,1)} %get-tuple-element.127.h1, bf16[2048,256]{1,0:T(8,128)(2,1)} %get-tuple-element.152.dq_a, bf16[2048,256]{1,0:T(8,128)(2,1)} %get-tuple-element.153.dk_a, ...), custom_call_target="tpu_custom_call" | custom-call | flops 171798688 | bytes 545259 | tf_op jit(solution)/shard_map/last/pallas_call | solution.py:1247
  255.2 9.5 %collective-permute-done.4 = bf16[448,512]{1,0:T(8,128)(2,1)} collective-permute-done((bf16[448,512]{1,0:T(8,128)(2,1)S(1)}, bf16[448,512]{1,0:T(8,128)(2,1)}, u32[]{:S(2)}, u32[]{:S(2)}) %collective-permute-start.4) | collective-permute-done | bytes 458784 | tf_op jit(solution)/shard_map/ppermute | solution.py:777
  270.3 6.6 %collective-permute-done.7 = bf16[224,512]{1,0:T(8,128)(2,1)S(1)} collective-permute-done((bf16[224,512]{1,0:T(8,128)(2,1)S(1)}, bf16[224,512]{1,0:T(8,128)(2,1)S(1)}, u32[]{:S(2)}, u32[]{:S(2)}) %collective-permute-start.7) | collective-permute-done | bytes 229408 | tf_op jit(solution)/shard_map/ppermute | solution.py:777
  285.5 8.4 %collective-permute-done.9 = bf16[2,56,512]{2,1,0:T(8,128)(2,1)S(1)} collective-permute-done((bf16[2,56,512]{2,1,0:T(8,128)(2,1)S(1)}, bf16[2,56,512]{2,1,0:T(8,128)(2,1)S(1)}, u32[]{:S(2)}, u32[]{:S(2)}) %collective-permute-start.9) | collective-permute-done | bytes 114720 | tf_op jit(solution)/shard_map/ppermute | solution.py:777
  299.7 7.0 %mlp_out.1 = (f32[512,2048]{1,0:T(8,128)}, f32[2048,512]{1,0:T(8,128)}) custom-call(s32[1]{0:T(128)} %bitcast.2.core, bf16[2,1024,512]{2,1,0:T(8,128)(2,1)} %bitcast.49, bf16[2,1024,512]{2,1,0:T(8,128)(2,1)} %copy-done.2), custom_call_target="tpu_custom_call" | custom-call | flops 1048576 | bytes 12582912 | tf_op jit(solution)/shard_map/mlp_out/pallas_call | solution.py:1307
  316.7 7.9 %collective-permute-done.17 = bf16[448,512]{1,0:T(8,128)(2,1)S(1)} collective-permute-done((bf16[448,512]{1,0:T(8,128)(2,1)S(1)}, bf16[448,512]{1,0:T(8,128)(2,1)S(1)}, u32[]{:S(2)}, u32[]{:S(2)}) %collective-permute-start.17) | collective-permute-done | bytes 458784 | tf_op jit(solution)/shard_map/ppermute | solution.py:777
  331.0 5.0 %rest_out.1 = (f32[512,1536]{1,0:T(8,128)}, f32[512,512]{1,0:T(8,128)}, f32[512,512]{1,0:T(8,128)}, f32[512,512]{1,0:T(8,128)}, f32[512]{0:T(512)}, /*index=5*/f...) custom-call(s32[1]{0:T(128)} %bitcast.2.core, bf16[2,896,512]{2,1,0:T(8,128)(2,1)} %copy-done.1, ...), custom_call_target="tpu_custom_call" | custom-call | flops 1048576 | bytes 12582912 | tf_op jit(solution)/shard_map/rest_out/pallas_call | solution.py:1335
  (102 shorter events, 67.4 us)
Async XLA Ops:
  1.7 21.4 %collective-permute-start = (bf16[512,512]{1,0:T(8,128)(2,1)S(1)}, bf16[512,512]{1,0:T(8,128)(2,1)S(1)}, u32[]{:S(2)}, u32[]{:S(2)}) collective-permute-start(bf16[512,512]{1,0:T(8,128)(2,1)S(1)} %slice.33), channel_id=1, source_target_pairs={{0,1},{1,2},{2,3},{4,5},{5,6},{6,7},{8,9},{9,10},{10,11},{12,13},{... | collective-permute-start | bytes 1572872 | tf_op jit(solution)/shard_map/ppermute | solution.py:928
  17.1 28.2 %all-to-all-start = ((f32[32,2,512]{2,1,0:T(2,128)}), f32[32,2,512]{2,1,0:T(2,128)S(1)}, u32[]{:S(2)}, u32[]{:S(2)}) async-start(f32[32,2,512]{2,1,0:T(2,128)} %get-tuple-element.120), calls=%async_computation | async-start | bytes 262144 | tf_op jit(solution)/shard_map/all_to_all | solution.py:126
  56.4 27.5 %all-to-all-start.1 = ((f32[32,2,512]{2,1,0:T(2,128)}), f32[32,2,512]{2,1,0:T(2,128)S(1)}, u32[]{:S(2)}, u32[]{:S(2)}) async-start(f32[32,2,512]{2,1,0:T(2,128)} %get-tuple-element.125), calls=%async_computation.1 | async-start | bytes 262144 | tf_op jit(solution)/shard_map/all_to_all | solution.py:126
  93.1 32.9 %all-to-all-start.2 = ((f32[32,2,512]{2,1,0:T(2,128)}), f32[32,2,512]{2,1,0:T(2,128)S(1)}, u32[]{:S(2)}, u32[]{:S(2)}) async-start(f32[32,2,512]{2,1,0:T(2,128)} %get-tuple-element.134), calls=%async_computation.2 | async-start | bytes 262144 | tf_op jit(solution)/shard_map/all_to_all | solution.py:126
  126.0 4.4 %collective-permute-start.1 = (bf16[2,1024,512]{2,1,0:T(8,128)(2,1)}, bf16[2,1024,512]{2,1,0:T(8,128)(2,1)S(1)}, u32[]{:S(2)}, u32[]{:S(2)}) collective-permute-start(bf16[2,1024,512]{2,1,0:T(8,128)(2,1)} %get-tuple-element.136), channel_id=1, source_target_pairs={{0,4},{4,0},{8,12},{12,8},{16,20},{20,16},{24,28},{28,24},{1,5},{5... | collective-permute-start | bytes 6291464 | tf_op jit(solution)/shard_map/ppermute | solution.py:777
  134.0 58.1 %all-to-all-start.3 = ((bf16[16,128,512]{2,1,0:T(8,128)(2,1)}), bf16[16,128,512]{2,1,0:T(8,128)(2,1)S(1)}, u32[]{:S(2)}, u32[]{:S(2)}) async-start(bf16[16,128,512]{2,1,0:T(8,128)(2,1)} %bitcast.3), calls=%async_computation.3 | async-start | bytes 4194304 | tf_op jit(solution)/shard_map/all_to_all | solution.py:772
  169.7 46.7 %collective-permute-start.2 = (bf16[2,512,512]{2,1,0:T(8,128)(2,1)}, bf16[2,512,512]{2,1,0:T(8,128)(2,1)S(1)}, u32[]{:S(2)}, u32[]{:S(2)}) collective-permute-start(bf16[2,512,512]{2,1,0:T(8,128)(2,1)} %get-tuple-element.165), channel_id=1, source_target_pairs={{1,0},{2,1},{3,2},{5,4},{6,5},{7,6},{9,8},{10,9},{11,10},{13,12},{... | collective-permute-start | bytes 3145736 | tf_op jit(solution)/shard_map/ppermute | solution.py:1185
  193.9 22.5 %all-to-all-start.4 = ((f32[32,2,512]{2,1,0:T(2,128)}), f32[32,2,512]{2,1,0:T(2,128)S(1)}, u32[]{:S(2)}, u32[]{:S(2)}) async-start(f32[32,2,512]{2,1,0:T(2,128)} %get-tuple-element.159), calls=%async_computation.4 | async-start | bytes 262144 | tf_op jit(solution)/shard_map/all_to_all | solution.py:126
  217.4 60.6 %all-to-all-start.5 = ((bf16[16,128,512]{2,1,0:T(8,128)(2,1)}), bf16[16,128,512]{2,1,0:T(8,128)(2,1)S(1)}, u32[]{:S(2)}, u32[]{:S(2)}) async-start(bf16[16,128,512]{2,1,0:T(8,128)(2,1)} %broadcast_in_dim.27), calls=%async_computation.5 | async-start | bytes 4194304 | tf_op jit(solution)/shard_map/all_to_all | solution.py:772
  251.7 12.9 %collective-permute-start.4 = (bf16[448,512]{1,0:T(8,128)(2,1)S(1)}, bf16[448,512]{1,0:T(8,128)(2,1)}, u32[]{:S(2)}, u32[]{:S(2)}) collective-permute-start(bf16[448,512]{1,0:T(8,128)(2,1)S(1)} %get-tuple-element.179), channel_id=1, source_target_pairs={{0,8},{4,12},{8,0},{12,4},{16,24},{20,28},{24,16},{28,20},{1,9},{5... | collective-permute-start | bytes 1376264 | tf_op jit(solution)/shard_map/ppermute | solution.py:777
  253.7 12.6 %collective-permute-start.5 = (bf16[448,512]{1,0:T(8,128)(2,1)}, bf16[448,512]{1,0:T(8,128)(2,1)}, u32[]{:S(2)}, u32[]{:S(2)}) collective-permute-start(bf16[448,512]{1,0:T(8,128)(2,1)} %get-tuple-element.180), channel_id=1, source_target_pairs={{0,16},{4,20},{8,24},{12,28},{16,0},{20,4},{24,8},{28,12},{1,17},{... | collective-permute-start | bytes 1376264 | tf_op jit(solution)/shard_map/ppermute | solution.py:777
  267.5 9.4 %collective-permute-start.7 = (bf16[224,512]{1,0:T(8,128)(2,1)S(1)}, bf16[224,512]{1,0:T(8,128)(2,1)S(1)}, u32[]{:S(2)}, u32[]{:S(2)}) collective-permute-start(bf16[224,512]{1,0:T(8,128)(2,1)S(1)} %get-tuple-element.182), channel_id=1, source_target_pairs={{0,8},{4,12},{8,0},{12,4},{16,24},{20,28},{24,16},{28,20},{1,9},{5... | collective-permute-start | bytes 688136 | tf_op jit(solution)/shard_map/ppermute | solution.py:777
  268.8 9.1 %collective-permute-start.6 = (bf16[224,512]{1,0:T(8,128)(2,1)S(1)}, bf16[224,512]{1,0:T(8,128)(2,1)S(1)}, u32[]{:S(2)}, u32[]{:S(2)}) collective-permute-start(bf16[224,512]{1,0:T(8,128)(2,1)S(1)} %get-tuple-element.181), channel_id=1, source_target_pairs={{0,16},{4,20},{8,24},{12,28},{16,0},{20,4},{24,8},{28,12},{1,17},{... | collective-permute-start | bytes 688136 | tf_op jit(solution)/shard_map/ppermute | solution.py:777
  278.1 15.9 %collective-permute-start.11 = (bf16[2,1024,512]{2,1,0:T(8,128)(2,1)S(1)}, bf16[2,1024,512]{2,1,0:T(8,128)(2,1)S(1)}, u32[]{:S(2)}, u32[]{:S(2)}) collective-permute-start(bf16[2,1024,512]{2,1,0:T(8,128)(2,1)S(1)} %bitcast.48), channel_id=1, source_target_pairs={{0,4},{4,0},{8,12},{12,8},{16,20},{20,16},{24,28},{28,24},{1,5},{5... | collective-permute-start | bytes 6291464 | tf_op jit(solution)/shard_map/ppermute | solution.py:777
  278.2 7.4 %collective-permute-start.10 = (bf16[2,56,512]{2,1,0:T(8,128)(2,1)S(1)}, bf16[2,56,512]{2,1,0:T(8,128)(2,1)S(1)}, u32[]{:S(2)}, u32[]{:S(2)}) collective-permute-start(bf16[2,56,512]{2,1,0:T(8,128)(2,1)S(1)} %pad_maximum_fusion.8), channel_id=1, source_target_pairs={{0,3},{1,2},{2,1},{3,0},{4,7},{5,6},{6,5},{7,4},{8,11},{9,10},{10,... | collective-permute-start | bytes 344072 | tf_op jit(solution)/shard_map/ppermute | solution.py:777
  281.6 12.3 %collective-permute-start.9 = (bf16[2,56,512]{2,1,0:T(8,128)(2,1)S(1)}, bf16[2,56,512]{2,1,0:T(8,128)(2,1)S(1)}, u32[]{:S(2)}, u32[]{:S(2)}) collective-permute-start(bf16[2,56,512]{2,1,0:T(8,128)(2,1)S(1)} %pad_maximum_fusion.7), channel_id=1, source_target_pairs={{0,2},{1,3},{2,0},{3,1},{4,6},{5,7},{6,4},{7,5},{8,10},{9,11},{10,... | collective-permute-start | bytes 344072 | tf_op jit(solution)/shard_map/ppermute | solution.py:777
  285.5 8.4 %collective-permute-start.8 = (bf16[2,56,512]{2,1,0:T(8,128)(2,1)S(1)}, bf16[2,56,512]{2,1,0:T(8,128)(2,1)S(1)}, u32[]{:S(2)}, u32[]{:S(2)}) collective-permute-start(bf16[2,56,512]{2,1,0:T(8,128)(2,1)S(1)} %pad_maximum_fusion.6), channel_id=1, source_target_pairs={{0,1},{1,0},{2,3},{3,2},{4,5},{5,4},{6,7},{7,6},{8,9},{9,8},{10,11... | collective-permute-start | bytes 344072 | tf_op jit(solution)/shard_map/ppermute | solution.py:777
  295.3 11.4 %collective-permute-start.12 = (bf16[2,56,512]{2,1,0:T(8,128)(2,1)S(1)}, bf16[2,56,512]{2,1,0:T(8,128)(2,1)S(1)}, u32[]{:S(2)}, u32[]{:S(2)}) collective-permute-start(bf16[2,56,512]{2,1,0:T(8,128)(2,1)S(1)} %add_convert_fusion.5), channel_id=1, source_target_pairs={{0,1},{1,0},{2,3},{3,2},{4,5},{5,4},{6,7},{7,6},{8,9},{9,8},{10,11... | collective-permute-start | bytes 344072 | tf_op jit(solution)/shard_map/ppermute | solution.py:777
  295.3 11.9 %collective-permute-start.13 = (bf16[2,56,512]{2,1,0:T(8,128)(2,1)S(1)}, bf16[2,56,512]{2,1,0:T(8,128)(2,1)S(1)}, u32[]{:S(2)}, u32[]{:S(2)}) collective-permute-start(bf16[2,56,512]{2,1,0:T(8,128)(2,1)S(1)} %add_convert_fusion.5), channel_id=1, source_target_pairs={{0,2},{1,3},{2,0},{3,1},{4,6},{5,7},{6,4},{7,5},{8,10},{9,11},{10,... | collective-permute-start | bytes 344072 | tf_op jit(solution)/shard_map/ppermute | solution.py:777
  298.3 8.9 %collective-permute-start.14 = (bf16[2,56,512]{2,1,0:T(8,128)(2,1)S(1)}, bf16[2,56,512]{2,1,0:T(8,128)(2,1)S(1)}, u32[]{:S(2)}, u32[]{:S(2)}) collective-permute-start(bf16[2,56,512]{2,1,0:T(8,128)(2,1)S(1)} %add_convert_fusion.5), channel_id=1, source_target_pairs={{0,3},{1,2},{2,1},{3,0},{4,7},{5,6},{6,5},{7,4},{8,11},{9,10},{10,... | collective-permute-start | bytes 344072 | tf_op jit(solution)/shard_map/ppermute | solution.py:777
  307.4 6.1 %collective-permute-start.15 = (bf16[224,512]{1,0:T(8,128)(2,1)S(1)}, bf16[224,512]{1,0:T(8,128)(2,1)S(1)}, u32[]{:S(2)}, u32[]{:S(2)}) collective-permute-start(bf16[224,512]{1,0:T(8,128)(2,1)S(1)} %get-tuple-element.196), channel_id=1, source_target_pairs={{0,16},{4,20},{8,24},{12,28},{16,0},{20,4},{24,8},{28,12},{1,17},{... | collective-permute-start | bytes 688136 | tf_op jit(solution)/shard_map/ppermute | solution.py:777
  308.7 6.0 %collective-permute-start.16 = (bf16[224,512]{1,0:T(8,128)(2,1)S(1)}, bf16[224,512]{1,0:T(8,128)(2,1)S(1)}, u32[]{:S(2)}, u32[]{:S(2)}) collective-permute-start(bf16[224,512]{1,0:T(8,128)(2,1)S(1)} %get-tuple-element.197), channel_id=1, source_target_pairs={{0,8},{4,12},{8,0},{12,4},{16,24},{20,28},{24,16},{28,20},{1,9},{5... | collective-permute-start | bytes 688136 | tf_op jit(solution)/shard_map/ppermute | solution.py:777
  314.8 9.8 %collective-permute-start.17 = (bf16[448,512]{1,0:T(8,128)(2,1)S(1)}, bf16[448,512]{1,0:T(8,128)(2,1)S(1)}, u32[]{:S(2)}, u32[]{:S(2)}) collective-permute-start(bf16[448,512]{1,0:T(8,128)(2,1)S(1)} %pad_maximum_fusion.4), channel_id=1, source_target_pairs={{0,8},{4,12},{8,0},{12,4},{16,24},{20,28},{24,16},{28,20},{1,9},{5... | collective-permute-start | bytes 1376264 | tf_op jit(solution)/shard_map/ppermute | solution.py:777
  316.1 9.4 %collective-permute-start.18 = (bf16[448,512]{1,0:T(8,128)(2,1)S(1)}, bf16[448,512]{1,0:T(8,128)(2,1)S(1)}, u32[]{:S(2)}, u32[]{:S(2)}) collective-permute-start(bf16[448,512]{1,0:T(8,128)(2,1)S(1)} %pad_maximum_fusion.5), channel_id=1, source_target_pairs={{0,16},{4,20},{8,24},{12,28},{16,0},{20,4},{24,8},{28,12},{1,17},{... | collective-permute-start | bytes 1376264 | tf_op jit(solution)/shard_map/ppermute | solution.py:777
  (15 other events, 70.7 us)
where the time goes:
time: 338 us; the launch traced here: 336 us
  Pallas kernels  193 us (57%)
  starting transfers between devices  66.5 us (20%)
  waiting for transfers between devices  53 us (16%)
  local copies, waits for them, and re-layouts  13.8 us (4%)
  other arithmetic  8.72 us (3%)
    ppermute x18, waiting for transfers between devices, swap(): return lax.ppermute(x, axis, [(i, i ^ bit) for i in range(n)])  48.6 us
    pallas_call x2, Pallas kernels, back_rest(): pl.pallas_call(back_rest_kernel, grid_spec=pltpu.PrefetchScalarGridSpec(n...  33.3 us
    pallas_call x1, Pallas kernels, body(): pl.pallas_call(mlp_back_kernel, grid=(blocks,), in_specs=[smem, rows_of(w...  26.9 us
    all_to_all x4, starting transfers between devices, exchange(): return lax.all_to_all(spread_rows, AXES, 0, 0, tiled=True)  24.4 us
    ppermute x18, starting transfers between devices, swap(): return lax.ppermute(x, axis, [(i, i ^ bit) for i in range(n)])  23 us
    pallas_call x1, Pallas kernels, body(): pl.pallas_call(attend_kernel, grid_spec=pltpu.PrefetchScalarGridSpec(num_...  21.3 us
    pallas_call x1, Pallas kernels, body(): pl.pallas_call(functools.partial(last_kernel, rows), grid=(blocks,), in_s...  21 us
    pallas_call x1, Pallas kernels, body(): pl.pallas_call(functools.partial(middle_kernel, rows), grid=(rows // MID_...  20.2 us
  transfers between devices with their start and end apart: 26, of which 14 were waited for; matrix products, arithmetic and copies ran while one was open for 3% of the time, Pallas kernels for 50%

commit v1 on v0

--- a/solution.py
+++ b/solution.py
@@ -13,7 +13,6 @@
 MID_TILE = 512
 HALF = 256
 PAIR = 128
-PAD = 128
 LATE_WEIGHT = 0.02
 EPS = 1e-05
 MASKED = -1e30
@@ -124,6 +123,10 @@
 
 def exchange(spread_rows):
     return lax.all_to_all(spread_rows, AXES, 0, 0, tiled=True)
+
+
+def near(array):
+    return pltpu.with_memory_space_constraint(array, pltpu.VMEM)
 
 
 def first_kernel(x, gain, bias, w_qkv, w_gate, h1, qkv, z1, stats, acc, z):
@@ -463,7 +466,7 @@
         dyt = dy * t
         dbranch[at, :] = dyt.astype(BF16)
         out = dy - dyt
-        gx[at, :] = out
+        gx[at, :] = out.astype(BF16)
         du = (out * t) * (branch - x[at, :].astype(F32))
         du1[at, :] = du.astype(BF16)
         sums_of.append(
@@ -507,8 +510,7 @@
     parts = [(slice(0, HALF), full), (slice(HALF, SPAN), slice(HALF, SPAN))]
     units = []
     for p in range(width // PAIR):
-        for s in range(2):
-            units += [(p, s, 0), (p, s, 1)] + ([(p, s, 2)] if wide else [])
+        units += [(p, 0), (p, 1)] + ([(p, 2)] if wide else [])
     held = {}
 
     def inputs(p):
@@ -529,37 +531,39 @@
         return held[p]
 
     def first(unit):
-        p, s, i = unit
+        p, i = unit
         e = inputs(p)
         ks, qs = (full, full) if i == 2 else parts[i]
         k, v, kt = e["before"] if i == 2 else e["own"]
-        q_s, d_s = e["q"][s][qs], e["do"][s][qs]
-        kt = kt[s * HD : (s + 1) * HD, ks]
-        return dot_nt(k[ks], q_s), dot_nt(v[ks], d_s), q_s, d_s, kt, ks, qs
+        q_s, d_s = [q[qs] for q in e["q"]], [d[qs] for d in e["do"]]
+        scores = [dot_nt(k[ks], q) for q in q_s]
+        dp = [dot_nt(v[ks], d) for d in d_s]
+        return scores, dp, q_s, d_s, kt[:, ks], ks, qs
 
     def second(unit, got):
-        p, s, i = unit
+        p, i = unit
         scores, dp, q_s, d_s, kt, ks, qs = got
         at = slice(p * PAIR, (p + 1) * PAIR)
-        x = jnp.exp(scores - lse[p, s : s + 1, qs])
-        if i == 0:
-            x = jnp.concatenate([jnp.where(mask, x[:, :HALF], 0.0), x[:, HALF:]], axis=1)
-        elif i == 1:
-            x = jnp.where(mask, x, 0.0)
-        ds = (x * (dp - delta[p, s : s + 1, qs])).astype(BF16)
-        dk, dv, dq = dot(ds, q_s), dot(x.astype(BF16), d_s), dot(kt, ds)
+        low_x, low_ds = [], []
+        for s in range(2):
+            x = jnp.exp(scores[s] - lse[p, s : s + 1, qs])
+            if i == 0:
+                x = jnp.concatenate([jnp.where(mask, x[:, :HALF], 0.0), x[:, HALF:]], axis=1)
+            elif i == 1:
+                x = jnp.where(mask, x, 0.0)
+            low_ds.append((x * (dp[s] - delta[p, s : s + 1, qs])).astype(BF16))
+            low_x.append(x.astype(BF16))
+            dq = dot(kt[s * HD : (s + 1) * HD, :], low_ds[s])
+            head = slice(p * PAIR + s * HD, p * PAIR + (s + 1) * HD)
+            if i == 0:
+                dq_t[head, :] = dq
+            else:
+                dq_t[head, qs] += dq
         target = carry if i == 2 else own
-        if s == 0:
-            target[0, ks, at] = dk
-            target[1, ks, at] = dv
-        else:
-            target[0, ks, at] += dk
-            target[1, ks, at] += dv
-        head = slice(p * PAIR + s * HD, p * PAIR + (s + 1) * HD)
-        if i == 0:
-            dq_t[head, :] = dq
-        else:
-            dq_t[head, qs] += dq
+        target[0, ks, at] = dot(
+            jnp.concatenate(low_ds, axis=1), jnp.concatenate(q_s, axis=0)
+        )
+        target[1, ks, at] = dot(jnp.concatenate(low_x, axis=1), jnp.concatenate(d_s, axis=0))
 
     in_turn(units, first, second)
 
@@ -708,7 +712,7 @@
     def norm(at, dh):
         n, r = normed(x[at, :].astype(F32))
         e = dh * lg
-        grad_x[at, :] = gx[at, :] + r * (
+        grad_x[at, :] = gx[at, :].astype(F32) + r * (
             e - jnp.mean(e, axis=-1, keepdims=True) - n * jnp.mean(e * n, axis=-1, keepdims=True)
         )
         sums_of.append([column_sum(dh * n), column_sum(dh)])
@@ -724,7 +728,8 @@
                 out[j // 2, (j % 2) * HALF : (j % 2 + 1) * HALF, :] = acc[j, at, :].astype(BF16)
             for j in range(2):
                 out[j, 2 * HALF : 3 * HALF, :] = g_mid[j, at, :]
-                out[j, 3 * HALF :, :] = jnp.zeros((PAD, width), BF16)
+                pad = out.shape[1] - 3 * HALF
+                out[j, 3 * HALF :, :] = jnp.zeros((pad, width), BF16)
         extra = side.shape[0]
         for out, mine in ((keep, core[0] == 0), (send, core[0] != 0)):
 
@@ -744,26 +749,31 @@
 
 
 def rest_out_kernel(core, mine, other, g_qkv, g_gate1, g_out, g_gate2, *vectors):
+    half = pl.program_id(0)
     width = g_out.shape[1]
     places = (
         ((g_qkv, 0), (g_qkv, 1), (g_gate2, 0)),
         ((g_qkv, 2), (g_gate1, 0), (g_out, 0)),
     )
-    for ref, half in ((mine, core[0]), (other, 1 - core[0])):
-        at = pl.ds(pl.multiple_of(half * HALF, HALF), HALF)
+
+    def write(ref):
         for lane, row_places in enumerate(places):
             for j, (out, column) in enumerate(row_places):
-                out[at, column * width : (column + 1) * width] = ref[
+                out[:, column * width : (column + 1) * width] = ref[
                     lane, j * HALF : (j + 1) * HALF, :
                 ].astype(F32)
-    a = mine[0, 3 * HALF : 3 * HALF + 16, :].astype(F32)
-    b = other[0, 3 * HALF : 3 * HALF + 16, :].astype(F32)
-    extra = jnp.where(core[0] == 0, a, b)
-    at = 0
-    for out in vectors:
-        for j in range(out.shape[0] // width):
-            out[j * width : (j + 1) * width] = extra[at]
-            at += 1
+
+        @pl.when(half == 0)
+        def _():
+            extra = ref[0, 3 * HALF : 3 * HALF + 16, :].astype(F32)
+            at = 0
+            for out in vectors:
+                for j in range(out.shape[0] // width):
+                    out[j * width : (j + 1) * width] = extra[at]
+                    at += 1
+
+    pl.when(core[0] == half)(functools.partial(write, mine))
+    pl.when(core[0] != half)(functools.partial(write, other))
 
 
 def between_chips(x):
@@ -997,7 +1007,7 @@
         compiler_params=params(VMEM_MIB),
         cost_estimate=cost(4 * mac, rows * width * 18, rows * width),
         name="mix",
-    )(att, tokens, z1, parts1, gate1_gain, gate1_shift, ln2_gain, ln2_bias, w_out, w_gate2)
+    )(att, tokens, z1, near(parts1), gate1_gain, gate1_shift, ln2_gain, ln2_bias, w_out, w_gate2)
     parts2 = exchange(stats2)
 
     act, slope, mlp = pl.pallas_call(
@@ -1035,7 +1045,7 @@
         compiler_params=params(VMEM_MIB),
         cost_estimate=cost(rows * width * 20, rows * width * 18, rows * width),
         name="gate2",
-    )(mlp, y1, z2, cotangent, parts2, gate2_gain, gate2_shift)
+    )(mlp, y1, z2, cotangent, near(parts2), gate2_gain, gate2_shift)
     parts_du2 = exchange(sums2)
 
     bias_rows = 1 + units // width
@@ -1062,12 +1072,12 @@
         ],
         out_shape=[
             struct((rows, width), BF16),
-            struct(mlp_half, BF16),
-            struct(mlp_half, BF16),
+            pltpu.VMEM(mlp_half, BF16),
+            pltpu.VMEM(mlp_half, BF16),
             struct((bias_rows, width), F32),
         ],
         scratch_shapes=[pltpu.VMEM((units, width), F32), pltpu.VMEM((width, units), F32)],
-        compiler_params=params(VMEM_MIB),
+        compiler_params=params(54),
         cost_estimate=cost(8 * rows * width * units, rows * units * 5),
         name="mlp_back",
     )(core, dmlp, act, slope, h2, w_up, w_down)
@@ -1100,7 +1110,7 @@
             whole((side_rows, width)),
         ],
         out_shape=[
-            struct((rows, width), F32),
+            struct((rows, width), BF16),
             struct((rows, width), BF16),
             struct((rows, width), BF16),
             struct((pairs, 2, rows), F32),
@@ -1130,9 +1140,9 @@
         tokens,
         z1,
         h2,
-        parts2,
-        parts_du2,
-        parts1,
+        near(parts2),
+        near(parts_du2),
+        near(parts1),
         gate2_gain,
         gate2_shift,
         gate1_gain,
@@ -1242,7 +1252,8 @@
     mine, parts_du1, back_b, arrived = lax.optimization_barrier((mine, parts_du1, back_b, arrived))
     gathered = between_chips(mine)
 
-    in_half = (2, 3 * HALF + PAD, width)
+    share = 4 * max(ndev // 2, 4)
+    in_half = (2, -(-(3 * HALF + 16) // share) * share, width)
     grouped = [rows_of(group, SPAN)] * 3 + [whole((2, SPAN, group))]
     grad_x, keep, send, g_sums = pl.pallas_call(
         functools.partial(last_kernel, rows),
@@ -1263,8 +1274,8 @@
         ],
         out_shape=[
             struct((rows, width), F32),
-            struct(in_half, BF16),
-            struct(in_half, BF16),
+            pltpu.VMEM(in_half, BF16),
+            pltpu.VMEM(in_half, BF16),
             struct((2, width), F32),
         ],
         scratch_shapes=[
@@ -1273,7 +1284,7 @@
             pltpu.VMEM((SPAN, 3 * width), BF16),
             pltpu.VMEM((2, width), F32),
         ],
-        compiler_params=params(VMEM_MIB),
+        compiler_params=params(54),
         cost_estimate=cost(LATE_WEIGHT * 16 * mac, LATE_WEIGHT * rows * width * 26),
         name="last",
     )(
@@ -1284,8 +1295,8 @@
         arrived,
         du1,
         z1,
-        parts1,
-        parts_du1,
+        near(parts1),
+        near(parts_du1),
         gate1_gain,
         g_mid,
         side,
@@ -1334,8 +1345,12 @@
         g_b_up,
     ) = pl.pallas_call(
         rest_out_kernel,
-        in_specs=[smem] + [pl.BlockSpec(memory_space=pltpu.VMEM)] * 2,
-        out_specs=[pl.BlockSpec(memory_space=pltpu.VMEM)] * 10,
+        grid=(2,),
+        in_specs=[smem] + [whole(in_half)] * 2,
+        out_specs=[pl.BlockSpec((HALF, 3 * width), lambda i: (i, 0))]
+        + [pl.BlockSpec((HALF, width), lambda i: (i, 0))] * 3
+        + [vec] * 5
+        + [whole((units,))],
         out_shape=[
             struct(w_qkv.shape, F32),
             struct(w_gate1.shape, F32),
@@ -1344,7 +1359,7 @@
         ]
         + [vector] * 5
         + [struct((units,), F32)],
-        compiler_params=pltpu.CompilerParams(vmem_limit_bytes=VMEM_MIB * MIB),
+        compiler_params=params(VMEM_MIB),
         cost_estimate=cost(units * width, 12 * MIB),
         name="rest_out",
     )(core, total.stacked, total.both)

time: 338 us -> 329 us (0.973)
  other arithmetic: 8.72 us -> 4.3 us
  local copies, waits for them, and re-layouts: 13.8 us -> 9.4 us
  transfers between devices with their start and end apart: 26 -> 26, of which waited for: 14 -> 14; matrix products, arithmetic and copies ran while one was open for 3% -> 2% of each run, Pallas kernels for 50% -> 51%
where the time goes in v1:
time: 329 us; the launch traced here: 327 us
  Pallas kernels  190 us (58%)
  starting transfers between devices  67.4 us (20%)
  waiting for transfers between devices  54.9 us (17%)
  local copies, waits for them, and re-layouts  9.4 us (3%)
  other arithmetic  4.3 us (1%)
    ppermute x18, waiting for transfers between devices, swap(): return lax.ppermute(x, axis, [(i, i ^ bit) for i in range(n)])  48.3 us
    pallas_call x2, Pallas kernels, back_rest(): pl.pallas_call(back_rest_kernel, grid_spec=pltpu.PrefetchScalarGridSpec(n...  32.8 us
    pallas_call x1, Pallas kernels, body(): pl.pallas_call(mlp_back_kernel, grid=(blocks,), in_specs=[smem, rows_of(w...  25.5 us
    all_to_all x4, starting transfers between devices, exchange(): return lax.all_to_all(spread_rows, AXES, 0, 0, tiled=True)  24.3 us
    ppermute x18, starting transfers between devices, swap(): return lax.ppermute(x, axis, [(i, i ^ bit) for i in range(n)])  22.8 us
    pallas_call x1, Pallas kernels, body(): pl.pallas_call(attend_kernel, grid_spec=pltpu.PrefetchScalarGridSpec(num_...  21.2 us
    pallas_call x1, Pallas kernels, body(): pl.pallas_call(functools.partial(last_kernel, rows), grid=(blocks,), in_s...  20.2 us
    pallas_call x1, Pallas kernels, body(): pl.pallas_call(mlp_kernel, grid=(blocks,), in_specs=[rows_of(width, SPAN)...  20.1 us
  transfers between devices with their start and end apart: 26, of which 14 were waited for; matrix products, arithmetic and copies ran while one was open for 2% of the time, Pallas kernels for 51%

profile of v1, /device:TPU:0, one launch (start us, length us, event | category | flops | bytes accessed | tf_op | source)
XLA Modules:
  0.0 327.3 jit_solution(4073799249402345644)
XLA Ops:
  1.7 5.0 %collective-permute-start = (bf16[512,512]{1,0:T(8,128)(2,1)S(1)}, bf16[512,512]{1,0:T(8,128)(2,1)S(1)}, u32[]{:S(2)}, u32[]{:S(2)}) collective-permute-start(bf16[512,512]{1,0:T(8,128)(2,1)S(1)} %slice.33), channel_id=1, source_target_pairs={{0,1},{1,2},{2,3},{4,5},{5,6},{6,7},{8,9},{9,10},{10,11},{12,13},{... | collective-permute-start | bytes 1572872 | tf_op jit(solution)/shard_map/ppermute | solution.py:938
  6.7 10.3 %first.1 = (bf16[2048,512]{1,0:T(8,128)(2,1)}, bf16[2048,1536]{1,0:T(8,128)(2,1)}, bf16[2048,512]{1,0:T(8,128)(2,1)}, f32[32,2,512]{2,1,0:T(2,128)}) custom-call(bf16[2048,512]{1,0:T(8,128)(2,1)} %x.7, f32[512]{0:T(512)} %ln_gain.5, f32[512]{0:T(512)} %bias.3, bf16[512,1536]{1,0:T(8,128)(2,1)} %w_qkv.5, bf16[512,512]{1,0:T(8,128)(2,1)} %w_gate1.1), custom_call_target="tpu_custom_call" | custom-call | flops 4294967296 | bytes 14680064 | tf_op jit(solution)/shard_map/first/pallas_call | solution.py:945
  17.1 5.1 %all-to-all-start = ((f32[32,2,512]{2,1,0:T(2,128)}), f32[32,2,512]{2,1,0:T(2,128)S(1)}, u32[]{:S(2)}, u32[]{:S(2)}) async-start(f32[32,2,512]{2,1,0:T(2,128)} %get-tuple-element.120), calls=%async_computation | async-start | bytes 262144 | tf_op jit(solution)/shard_map/all_to_all | solution.py:125
  23.9 21.2 %attend.1 = (bf16[2048,512]{1,0:T(8,128)(2,1)}, f32[4,2,2048]{2,1,0:T(2,128)}, bf16[512,1024]{1,0:T(8,128)(2,1)}) custom-call(s32[4]{0:T(128)} %dynamic_slice.99.flags, bf16[2048,1536]{1,0:T(8,128)(2,1)} %get-tuple-element.117.qkv.prev.q.k.v.kp.vp, bf16[2048,1536]{1,0:T(8,128)(2,1)} %get-tuple-element.117.qkv.prev.q.k.v.kp.vp, bf16[512,512]{1,0:T(8,128)(2,1)} %copy-done.7, ...), custom_call_target="tpu_custom_call" | custom-call | flops 10737418240 | bytes 12582912 | tf_op jit(solution)/shard_map/attend/pallas_call | solution.py:963
  45.2 10.5 %mix.1 = (f32[2048,512]{1,0:T(8,128)}, bf16[2048,512]{1,0:T(8,128)(2,1)}, f32[2048,512]{1,0:T(8,128)}, f32[32,2,512]{2,1,0:T(2,128)}) custom-call(bf16[2048,512]{1,0:T(8,128)(2,1)} %get-tuple-element.118.att, bf16[2048,512]{1,0:T(8,128)(2,1)} %x.7, bf16[2048,512]{1,0:T(8,128)(2,1)} %get-tuple-element.119.z1, f32[32,2,512]{2,1,0:T(2,128)S(1)} %all-to-all-done.parts.parts1, ...), custom_call_target="tpu_custom_call" | custom-call | flops 2147483648 | bytes 18874368 | tf_op jit(solution)/shard_map/mix/pallas_call | solution.py:993
  55.7 6.5 %all-to-all-start.1 = ((f32[32,2,512]{2,1,0:T(2,128)}), f32[32,2,512]{2,1,0:T(2,128)S(1)}, u32[]{:S(2)}, u32[]{:S(2)}) async-start(f32[32,2,512]{2,1,0:T(2,128)} %get-tuple-element.125), calls=%async_computation.1 | async-start | bytes 262144 | tf_op jit(solution)/shard_map/all_to_all | solution.py:125
  62.2 20.1 %mlp.1 = (bf16[2048,2048]{1,0:T(8,128)(2,1)}, bf16[2048,2048]{1,0:T(8,128)(2,1)}, f32[2048,512]{1,0:T(8,128)}) custom-call(bf16[2048,512]{1,0:T(8,128)(2,1)} %get-tuple-element.121.h2, bf16[512,2048]{1,0:T(8,128)(2,1)} %w_up.3, f32[2048]{0:T(1024)} %b_up.1, bf16[2048,512]{1,0:T(8,128)(2,1)} %w_down.3, f32[512]{0:T(512)} %b_down.1), custom_call_target="tpu_custom_call" | custom-call | flops 8589934592 | bytes 16777216 | tf_op jit(solution)/shard_map/mlp/pallas_call | solution.py:1013
  82.3 8.9 %gate2.1 = (bf16[2048,512]{1,0:T(8,128)(2,1)}, bf16[2048,512]{1,0:T(8,128)(2,1)}, f32[32,2,512]{2,1,0:T(2,128)}) custom-call(f32[2048,512]{1,0:T(8,128)} %get-tuple-element.122.mlp, f32[2048,512]{1,0:T(8,128)} %get-tuple-element.123.y1, f32[2048,512]{1,0:T(8,128)} %get-tuple-element.124.z2, bf16[2048,512]{1,0:T(8,128)(2,1)} %c.3, ...), custom_call_target="tpu_custom_call" | custom-call | flops 20971520 | bytes 18874368 | tf_op jit(solution)/shard_map/gate2/pallas_call | solution.py:1034
  91.1 6.0 %all-to-all-start.2 = ((f32[32,2,512]{2,1,0:T(2,128)}), f32[32,2,512]{2,1,0:T(2,128)S(1)}, u32[]{:S(2)}, u32[]{:S(2)}) async-start(f32[32,2,512]{2,1,0:T(2,128)} %get-tuple-element.134), calls=%async_computation.2 | async-start | bytes 262144 | tf_op jit(solution)/shard_map/all_to_all | solution.py:125
  97.1 25.5 %mlp_back.1 = (bf16[2048,512]{1,0:T(8,128)(2,1)}, bf16[2,1024,512]{2,1,0:T(8,128)(2,1)S(1)}, bf16[2,1024,512]{2,1,0:T(8,128)(2,1)S(1)}, f32[5,512]{1,0:T(8,128)}) custom-call(s32[1]{0:T(128)} %bitcast.2.core, bf16[2048,512]{1,0:T(8,128)(2,1)} %get-tuple-element.128.dmlp, bf16[2048,2048]{1,0:T(8,128)(2,1)} %get-tuple-element.129.act, ...), custom_call_target="tpu_custom_call" | custom-call | flops 17179869184 | bytes 20971520 | tf_op jit(solution)/shard_map/mlp_back/pallas_call | solution.py:1055
  130.3 6.8 %all-to-all-start.3 = ((bf16[16,128,512]{2,1,0:T(8,128)(2,1)}), bf16[16,128,512]{2,1,0:T(8,128)(2,1)S(1)}, u32[]{:S(2)}, u32[]{:S(2)}) async-start(bf16[16,128,512]{2,1,0:T(8,128)(2,1)} %bitcast.48), calls=%async_computation.3 | async-start | bytes 4194304 | tf_op jit(solution)/shard_map/all_to_all | solution.py:782
  137.2 20.1 %middle.1 = (bf16[2048,512]{1,0:T(8,128)(2,1)}, bf16[2048,512]{1,0:T(8,128)(2,1)}, bf16[2048,512]{1,0:T(8,128)(2,1)}, f32[4,2,2048]{2,1,0:T(2,128)}, bf16[2,512,...) custom-call(bf16[2048,512]{1,0:T(8,128)(2,1)} %c.3, ...), custom_call_target="tpu_custom_call" | custom-call | flops 5368709120 | bytes 39845888 | tf_op jit(solution)/shard_map/middle/pallas_call | solution.py:1095
  157.2 8.4 %attend_back_first.1 = (bf16[512,512]{1,0:T(8,128)(2,1)}, f32[2,512,512]{2,1,0:T(8,128)}, bf16[2,512,512]{2,1,0:T(8,128)(2,1)}) custom-call(s32[4]{0:T(128)} %dynamic_slice.99.flags, bf16[2048,1536]{1,0:T(8,128)(2,1)} %get-tuple-element.117.qkv.prev.q.k.v.kp.vp, bf16[2048,1536]{1,0:T(8,128)(2,1)} %get-tuple-element.117.qkv.prev.q.k.v.kp.vp, ...), custom_call_target="tpu_custom_call" | custom-call | flops 5368709120 | bytes 8388608 | tf_op jit(solution)/shard_map/attend_back_first/pallas_call | solution.py:1159
  166.9 16.4 %attend_back_rest.2 = (bf16[2048,256]{1,0:T(8,128)(2,1)}, bf16[2048,256]{1,0:T(8,128)(2,1)}, bf16[2048,256]{1,0:T(8,128)(2,1)}, f32[2,512,256]{2,1,0:T(8,128)}) custom-call(s32[4]{0:T(128)} %dynamic_slice.99.flags, bf16[2048,1536]{1,0:T(8,128)(2,1)} %get-tuple-element.117.qkv.prev.q.k.v.kp.vp, bf16[2048,1536]{1,0:T(8,128)(2,1)} %get-tuple-element.117.qkv.prev.q.k.v.kp.vp, ...), custom_call_target="tpu_custom_call" | custom-call | flops 8053063680 | bytes 10485760 | tf_op jit(solution)/shard_map/attend_back_rest/pallas_call | solution.py:1211
  183.4 5.0 %all-to-all-done.3 = bf16[16,128,512]{2,1,0:T(8,128)(2,1)S(1)} async-done(((bf16[16,128,512]{2,1,0:T(8,128)(2,1)}), bf16[16,128,512]{2,1,0:T(8,128)(2,1)S(1)}, u32[]{:S(2)}, u32[]{:S(2)}) %all-to-all-start.3) | async-done | bytes 2097184 | tf_op jit(solution)/shard_map/all_to_all | solution.py:782
  190.2 6.8 %all-to-all-start.4 = ((f32[32,2,512]{2,1,0:T(2,128)}), f32[32,2,512]{2,1,0:T(2,128)S(1)}, u32[]{:S(2)}, u32[]{:S(2)}) async-start(f32[32,2,512]{2,1,0:T(2,128)} %get-tuple-element.159), calls=%async_computation.4 | async-start | bytes 262144 | tf_op jit(solution)/shard_map/all_to_all | solution.py:125
  197.0 16.4 %attend_back_rest.3 = (bf16[2048,256]{1,0:T(8,128)(2,1)}, bf16[2048,256]{1,0:T(8,128)(2,1)}, bf16[2048,256]{1,0:T(8,128)(2,1)}, f32[2,512,256]{2,1,0:T(8,128)}) custom-call(s32[4]{0:T(128)} %dynamic_slice.99.flags, bf16[2048,1536]{1,0:T(8,128)(2,1)} %get-tuple-element.117.qkv.prev.q.k.v.kp.vp, bf16[2048,1536]{1,0:T(8,128)(2,1)} %get-tuple-element.117.qkv.prev.q.k.v.kp.vp, ...), custom_call_target="tpu_custom_call" | custom-call | flops 161061280 | bytes 209715 | tf_op jit(solution)/shard_map/attend_back_rest/pallas_call | solution.py:1211
  214.4 7.2 %all-to-all-start.5 = ((bf16[16,128,512]{2,1,0:T(8,128)(2,1)}), bf16[16,128,512]{2,1,0:T(8,128)(2,1)}, u32[]{:S(2)}, u32[]{:S(2)}) async-start(bf16[16,128,512]{2,1,0:T(8,128)(2,1)} %broadcast_in_dim.27), calls=%async_computation.5 | async-start | bytes 4194304 | tf_op jit(solution)/shard_map/all_to_all | solution.py:782
  221.6 20.2 %last.1 = (f32[2048,512]{1,0:T(8,128)}, bf16[2,832,512]{2,1,0:T(8,128)(2,1)S(1)}, bf16[2,832,512]{2,1,0:T(8,128)(2,1)}, f32[2,512]{1,0:T(2,128)}) custom-call(s32[1]{0:T(128)} %bitcast.2.core, bf16[2048,512]{1,0:T(8,128)(2,1)} %get-tuple-element.127.h1, bf16[2048,256]{1,0:T(8,128)(2,1)} %get-tuple-element.152.dq_a, ...), custom_call_target="tpu_custom_call" | custom-call | flops 171798688 | bytes 545259 | tf_op jit(solution)/shard_map/last/pallas_call | solution.py:1258
  249.9 9.4 %collective-permute-done.4 = bf16[416,512]{1,0:T(8,128)(2,1)S(1)} collective-permute-done((bf16[416,512]{1,0:T(8,128)(2,1)S(1)}, bf16[416,512]{1,0:T(8,128)(2,1)S(1)}, u32[]{:S(2)}, u32[]{:S(2)}) %collective-permute-start.4) | collective-permute-done | bytes 426016 | tf_op jit(solution)/shard_map/ppermute | solution.py:787
  262.5 6.1 %collective-permute-done.7 = bf16[208,512]{1,0:T(8,128)(2,1)S(1)} collective-permute-done((bf16[208,512]{1,0:T(8,128)(2,1)S(1)}, bf16[208,512]{1,0:T(8,128)(2,1)S(1)}, u32[]{:S(2)}, u32[]{:S(2)}) %collective-permute-start.7) | collective-permute-done | bytes 213024 | tf_op jit(solution)/shard_map/ppermute | solution.py:787
  279.5 8.4 %collective-permute-done.9 = bf16[2,52,512]{2,1,0:T(8,128)(2,1)S(1)} collective-permute-done((bf16[2,52,512]{2,1,0:T(8,128)(2,1)S(1)}, bf16[2,52,512]{2,1,0:T(8,128)(2,1)S(1)}, u32[]{:S(2)}, u32[]{:S(2)}) %collective-permute-start.9) | collective-permute-done | bytes 106528 | tf_op jit(solution)/shard_map/ppermute | solution.py:787
  292.5 7.0 %mlp_out.1 = (f32[512,2048]{1,0:T(8,128)}, f32[2048,512]{1,0:T(8,128)}) custom-call(s32[1]{0:T(128)} %bitcast.2.core, bf16[2,1024,512]{2,1,0:T(8,128)(2,1)} %bitcast.18.mine, bf16[2,1024,512]{2,1,0:T(8,128)(2,1)} %copy-done.2), custom_call_target="tpu_custom_call" | custom-call | flops 1048576 | bytes 12582912 | tf_op jit(solution)/shard_map/mlp_out/pallas_call | solution.py:1318
  309.2 7.7 %collective-permute-done.17 = bf16[416,512]{1,0:T(8,128)(2,1)S(1)} collective-permute-done((bf16[416,512]{1,0:T(8,128)(2,1)S(1)}, bf16[416,512]{1,0:T(8,128)(2,1)S(1)}, u32[]{:S(2)}, u32[]{:S(2)}) %collective-permute-start.17) | collective-permute-done | bytes 426016 | tf_op jit(solution)/shard_map/ppermute | solution.py:787
  (94 shorter events, 61.0 us)
Async XLA Ops:
  1.7 21.4 %collective-permute-start = (bf16[512,512]{1,0:T(8,128)(2,1)S(1)}, bf16[512,512]{1,0:T(8,128)(2,1)S(1)}, u32[]{:S(2)}, u32[]{:S(2)}) collective-permute-start(bf16[512,512]{1,0:T(8,128)(2,1)S(1)} %slice.33), channel_id=1, source_target_pairs={{0,1},{1,2},{2,3},{4,5},{5,6},{6,7},{8,9},{9,10},{10,11},{12,13},{... | collective-permute-start | bytes 1572872 | tf_op jit(solution)/shard_map/ppermute | solution.py:938
  17.1 28.1 %all-to-all-start = ((f32[32,2,512]{2,1,0:T(2,128)}), f32[32,2,512]{2,1,0:T(2,128)S(1)}, u32[]{:S(2)}, u32[]{:S(2)}) async-start(f32[32,2,512]{2,1,0:T(2,128)} %get-tuple-element.120), calls=%async_computation | async-start | bytes 262144 | tf_op jit(solution)/shard_map/all_to_all | solution.py:125
  55.7 26.6 %all-to-all-start.1 = ((f32[32,2,512]{2,1,0:T(2,128)}), f32[32,2,512]{2,1,0:T(2,128)S(1)}, u32[]{:S(2)}, u32[]{:S(2)}) async-start(f32[32,2,512]{2,1,0:T(2,128)} %get-tuple-element.125), calls=%async_computation.1 | async-start | bytes 262144 | tf_op jit(solution)/shard_map/all_to_all | solution.py:125
  91.1 32.8 %all-to-all-start.2 = ((f32[32,2,512]{2,1,0:T(2,128)}), f32[32,2,512]{2,1,0:T(2,128)S(1)}, u32[]{:S(2)}, u32[]{:S(2)}) async-start(f32[32,2,512]{2,1,0:T(2,128)} %get-tuple-element.134), calls=%async_computation.2 | async-start | bytes 262144 | tf_op jit(solution)/shard_map/all_to_all | solution.py:125
  124.0 4.4 %collective-permute-start.1 = (bf16[2,1024,512]{2,1,0:T(8,128)(2,1)}, bf16[2,1024,512]{2,1,0:T(8,128)(2,1)S(1)}, u32[]{:S(2)}, u32[]{:S(2)}) collective-permute-start(bf16[2,1024,512]{2,1,0:T(8,128)(2,1)} %copy-done), channel_id=1, source_target_pairs={{0,4},{4,0},{8,12},{12,8},{16,20},{20,16},{24,28},{28,24},{1,5},{5... | collective-permute-start | bytes 6291464 | tf_op jit(solution)/shard_map/ppermute | solution.py:787
  130.3 58.1 %all-to-all-start.3 = ((bf16[16,128,512]{2,1,0:T(8,128)(2,1)}), bf16[16,128,512]{2,1,0:T(8,128)(2,1)S(1)}, u32[]{:S(2)}, u32[]{:S(2)}) async-start(bf16[16,128,512]{2,1,0:T(8,128)(2,1)} %bitcast.48), calls=%async_computation.3 | async-start | bytes 4194304 | tf_op jit(solution)/shard_map/all_to_all | solution.py:782
  165.7 47.7 %collective-permute-start.2 = (bf16[2,512,512]{2,1,0:T(8,128)(2,1)}, bf16[2,512,512]{2,1,0:T(8,128)(2,1)S(1)}, u32[]{:S(2)}, u32[]{:S(2)}) collective-permute-start(bf16[2,512,512]{2,1,0:T(8,128)(2,1)} %get-tuple-element.165), channel_id=1, source_target_pairs={{1,0},{2,1},{3,2},{5,4},{6,5},{7,6},{9,8},{10,9},{11,10},{13,12},{... | collective-permute-start | bytes 3145736 | tf_op jit(solution)/shard_map/ppermute | solution.py:1195
  190.2 23.2 %all-to-all-start.4 = ((f32[32,2,512]{2,1,0:T(2,128)}), f32[32,2,512]{2,1,0:T(2,128)S(1)}, u32[]{:S(2)}, u32[]{:S(2)}) async-start(f32[32,2,512]{2,1,0:T(2,128)} %get-tuple-element.159), calls=%async_computation.4 | async-start | bytes 262144 | tf_op jit(solution)/shard_map/all_to_all | solution.py:125
  214.4 56.6 %all-to-all-start.5 = ((bf16[16,128,512]{2,1,0:T(8,128)(2,1)}), bf16[16,128,512]{2,1,0:T(8,128)(2,1)}, u32[]{:S(2)}, u32[]{:S(2)}) async-start(bf16[16,128,512]{2,1,0:T(8,128)(2,1)} %broadcast_in_dim.27), calls=%async_computation.5 | async-start | bytes 4194304 | tf_op jit(solution)/shard_map/all_to_all | solution.py:782
  246.3 12.9 %collective-permute-start.4 = (bf16[416,512]{1,0:T(8,128)(2,1)S(1)}, bf16[416,512]{1,0:T(8,128)(2,1)S(1)}, u32[]{:S(2)}, u32[]{:S(2)}) collective-permute-start(bf16[416,512]{1,0:T(8,128)(2,1)S(1)} %get-tuple-element.179), channel_id=1, source_target_pairs={{0,8},{4,12},{8,0},{12,4},{16,24},{20,28},{24,16},{28,20},{1,9},{5... | collective-permute-start | bytes 1277960 | tf_op jit(solution)/shard_map/ppermute | solution.py:787
  248.4 11.6 %collective-permute-start.5 = (bf16[416,512]{1,0:T(8,128)(2,1)S(1)}, bf16[416,512]{1,0:T(8,128)(2,1)S(1)}, u32[]{:S(2)}, u32[]{:S(2)}) collective-permute-start(bf16[416,512]{1,0:T(8,128)(2,1)S(1)} %get-tuple-element.180), channel_id=1, source_target_pairs={{0,16},{4,20},{8,24},{12,28},{16,0},{20,4},{24,8},{28,12},{1,17},{... | collective-permute-start | bytes 1277960 | tf_op jit(solution)/shard_map/ppermute | solution.py:787
  260.1 8.5 %collective-permute-start.7 = (bf16[208,512]{1,0:T(8,128)(2,1)S(1)}, bf16[208,512]{1,0:T(8,128)(2,1)S(1)}, u32[]{:S(2)}, u32[]{:S(2)}) collective-permute-start(bf16[208,512]{1,0:T(8,128)(2,1)S(1)} %get-tuple-element.182), channel_id=1, source_target_pairs={{0,8},{4,12},{8,0},{12,4},{16,24},{20,28},{24,16},{28,20},{1,9},{5... | collective-permute-start | bytes 638984 | tf_op jit(solution)/shard_map/ppermute | solution.py:787
  261.4 7.9 %collective-permute-start.6 = (bf16[208,512]{1,0:T(8,128)(2,1)S(1)}, bf16[208,512]{1,0:T(8,128)(2,1)S(1)}, u32[]{:S(2)}, u32[]{:S(2)}) collective-permute-start(bf16[208,512]{1,0:T(8,128)(2,1)S(1)} %get-tuple-element.181), channel_id=1, source_target_pairs={{0,16},{4,20},{8,24},{12,28},{16,0},{20,4},{24,8},{28,12},{1,17},{... | collective-permute-start | bytes 638984 | tf_op jit(solution)/shard_map/ppermute | solution.py:787
  271.0 17.0 %collective-permute-start.11 = (bf16[2,1024,512]{2,1,0:T(8,128)(2,1)}, bf16[2,1024,512]{2,1,0:T(8,128)(2,1)S(1)}, u32[]{:S(2)}, u32[]{:S(2)}) collective-permute-start(bf16[2,1024,512]{2,1,0:T(8,128)(2,1)} %bitcast.18.mine), channel_id=1, source_target_pairs={{0,4},{4,0},{8,12},{12,8},{16,20},{20,16},{24,28},{28,24},{1,5},{5... | collective-permute-start | bytes 6291464 | tf_op jit(solution)/shard_map/ppermute | solution.py:787
  271.0 8.6 %collective-permute-start.10 = (bf16[2,52,512]{2,1,0:T(8,128)(2,1)S(1)}, bf16[2,52,512]{2,1,0:T(8,128)(2,1)S(1)}, u32[]{:S(2)}, u32[]{:S(2)}) collective-permute-start(bf16[2,52,512]{2,1,0:T(8,128)(2,1)S(1)} %pad_maximum_fusion.8), channel_id=1, source_target_pairs={{0,3},{1,2},{2,1},{3,0},{4,7},{5,6},{6,5},{7,4},{8,11},{9,10},{10,... | collective-permute-start | bytes 319496 | tf_op jit(solution)/shard_map/ppermute | solution.py:787
  275.5 12.4 %collective-permute-start.9 = (bf16[2,52,512]{2,1,0:T(8,128)(2,1)S(1)}, bf16[2,52,512]{2,1,0:T(8,128)(2,1)S(1)}, u32[]{:S(2)}, u32[]{:S(2)}) collective-permute-start(bf16[2,52,512]{2,1,0:T(8,128)(2,1)S(1)} %pad_maximum_fusion.7), channel_id=1, source_target_pairs={{0,2},{1,3},{2,0},{3,1},{4,6},{5,7},{6,4},{7,5},{8,10},{9,11},{10,... | collective-permute-start | bytes 319496 | tf_op jit(solution)/shard_map/ppermute | solution.py:787
  279.5 8.4 %collective-permute-start.8 = (bf16[2,52,512]{2,1,0:T(8,128)(2,1)S(1)}, bf16[2,52,512]{2,1,0:T(8,128)(2,1)S(1)}, u32[]{:S(2)}, u32[]{:S(2)}) collective-permute-start(bf16[2,52,512]{2,1,0:T(8,128)(2,1)S(1)} %pad_maximum_fusion.6), channel_id=1, source_target_pairs={{0,1},{1,0},{2,3},{3,2},{4,5},{5,4},{6,7},{7,6},{8,9},{9,8},{10,11... | collective-permute-start | bytes 319496 | tf_op jit(solution)/shard_map/ppermute | solution.py:787
  288.0 11.4 %collective-permute-start.12 = (bf16[2,52,512]{2,1,0:T(8,128)(2,1)S(1)}, bf16[2,52,512]{2,1,0:T(8,128)(2,1)S(1)}, u32[]{:S(2)}, u32[]{:S(2)}) collective-permute-start(bf16[2,52,512]{2,1,0:T(8,128)(2,1)S(1)} %add_convert_fusion.5), channel_id=1, source_target_pairs={{0,1},{1,0},{2,3},{3,2},{4,5},{5,4},{6,7},{7,6},{8,9},{9,8},{10,11... | collective-permute-start | bytes 319496 | tf_op jit(solution)/shard_map/ppermute | solution.py:787
  288.1 11.9 %collective-permute-start.13 = (bf16[2,52,512]{2,1,0:T(8,128)(2,1)S(1)}, bf16[2,52,512]{2,1,0:T(8,128)(2,1)S(1)}, u32[]{:S(2)}, u32[]{:S(2)}) collective-permute-start(bf16[2,52,512]{2,1,0:T(8,128)(2,1)S(1)} %add_convert_fusion.5), channel_id=1, source_target_pairs={{0,2},{1,3},{2,0},{3,1},{4,6},{5,7},{6,4},{7,5},{8,10},{9,11},{10,... | collective-permute-start | bytes 319496 | tf_op jit(solution)/shard_map/ppermute | solution.py:787
  290.9 9.1 %collective-permute-start.14 = (bf16[2,52,512]{2,1,0:T(8,128)(2,1)S(1)}, bf16[2,52,512]{2,1,0:T(8,128)(2,1)S(1)}, u32[]{:S(2)}, u32[]{:S(2)}) collective-permute-start(bf16[2,52,512]{2,1,0:T(8,128)(2,1)S(1)} %add_convert_fusion.5), channel_id=1, source_target_pairs={{0,3},{1,2},{2,1},{3,0},{4,7},{5,6},{6,5},{7,4},{8,11},{9,10},{10,... | collective-permute-start | bytes 319496 | tf_op jit(solution)/shard_map/ppermute | solution.py:787
  300.2 5.9 %collective-permute-start.15 = (bf16[208,512]{1,0:T(8,128)(2,1)S(1)}, bf16[208,512]{1,0:T(8,128)(2,1)S(1)}, u32[]{:S(2)}, u32[]{:S(2)}) collective-permute-start(bf16[208,512]{1,0:T(8,128)(2,1)S(1)} %get-tuple-element.196), channel_id=1, source_target_pairs={{0,16},{4,20},{8,24},{12,28},{16,0},{20,4},{24,8},{28,12},{1,17},{... | collective-permute-start | bytes 638984 | tf_op jit(solution)/shard_map/ppermute | solution.py:787
  301.9 5.9 %collective-permute-start.16 = (bf16[208,512]{1,0:T(8,128)(2,1)S(1)}, bf16[208,512]{1,0:T(8,128)(2,1)S(1)}, u32[]{:S(2)}, u32[]{:S(2)}) collective-permute-start(bf16[208,512]{1,0:T(8,128)(2,1)S(1)} %get-tuple-element.197), channel_id=1, source_target_pairs={{0,8},{4,12},{8,0},{12,4},{16,24},{20,28},{24,16},{28,20},{1,9},{5... | collective-permute-start | bytes 638984 | tf_op jit(solution)/shard_map/ppermute | solution.py:787
  307.8 9.0 %collective-permute-start.17 = (bf16[416,512]{1,0:T(8,128)(2,1)S(1)}, bf16[416,512]{1,0:T(8,128)(2,1)S(1)}, u32[]{:S(2)}, u32[]{:S(2)}) collective-permute-start(bf16[416,512]{1,0:T(8,128)(2,1)S(1)} %pad_maximum_fusion.4), channel_id=1, source_target_pairs={{0,8},{4,12},{8,0},{12,4},{16,24},{20,28},{24,16},{28,20},{1,9},{5... | collective-permute-start | bytes 1277960 | tf_op jit(solution)/shard_map/ppermute | solution.py:787
  308.3 8.7 %collective-permute-start.18 = (bf16[416,512]{1,0:T(8,128)(2,1)S(1)}, bf16[416,512]{1,0:T(8,128)(2,1)S(1)}, u32[]{:S(2)}, u32[]{:S(2)}) collective-permute-start(bf16[416,512]{1,0:T(8,128)(2,1)S(1)} %pad_maximum_fusion.5), channel_id=1, source_target_pairs={{0,16},{4,20},{8,24},{12,28},{16,0},{20,4},{24,8},{28,12},{1,17},{... | collective-permute-start | bytes 1277960 | tf_op jit(solution)/shard_map/ppermute | solution.py:787
  (11 other events, 42.5 us)
